TPU v7x, 32 devices: a whole 2x2x4 slice. The times are simulated.
32 devices in a mesh: dp: 16 (over z, y, core), mp: 2 (over x).
Axes of the slice: x: 2, y: 2, z: 4, core: 2. Of those that a mesh axis runs over, the one named last changes fastest.
Arguments:
- tokens: bfloat16 [256, 6144], P('dp', 'mp'), may hold values from -6 to 6
- norm_gain: float32 [6144], P('mp'), may hold values from 0.25 to 1.75
- w_up: bfloat16 [6144, 24576], P('mp', 'dp'), may hold values from -0.078125 to 0.078125
- cotangent: bfloat16 [256, 24576], P('mp', 'dp'), may hold values from -32 to 32
Outputs:
- sharp_grad: float32 [6144, 24576], P('mp', 'dp')
All inputs are finite; a program needn't handle non-finite values.
Results may differ from a plain program's by a relative error of at most 0.0048.
Values may be sent and summed in bfloat16 or wider, within the bound.
A program may use at most 64 MiB of HBM per device.

v0:
```python
import math

import jax
import jax.numpy as jnp
from jax import lax
from jax.sharding import PartitionSpec as P

FF = 24576


def gelu_slope(value):
    cdf = 0.5 * (1.0 + lax.erf(value * (1.0 / math.sqrt(2.0))))
    dens = jnp.exp(-0.5 * value * value) * (1.0 / math.sqrt(2.0 * math.pi))
    return cdf + value * dens


def per_device(tokens, norm_gain, w_up, cotangent):
    values = tokens.astype(jnp.float32)
    width = values.shape[1] * lax.axis_size("mp")
    total, squares = lax.psum((jnp.sum(values, axis=1), jnp.sum(values * values, axis=1)), "mp")
    mean = total / width
    var = squares / width - mean * mean
    normed = (
        (values - mean[:, None]) * lax.rsqrt(var[:, None] + 1e-06) * norm_gain[None, :]
    ).astype(jnp.bfloat16)
    token_count = tokens.shape[0] * lax.axis_size("dp")
    scale = 1.0 / math.sqrt(token_count)

    def project(weights):
        return jnp.dot(
            lax.all_gather(normed, "dp", axis=0, tiled=True),
            weights,
            preferred_element_type=jnp.float32,
        )

    def backproject(slope_all):
        return lax.dot_general(
            lax.all_gather(normed, "dp", axis=0, tiled=True),
            slope_all,
            (((0,), (0,)), ((), ())),
            preferred_element_type=jnp.float32,
        )

    def weight_grad(weights):
        partial_pre = project(weights)
        pre = lax.psum_scatter(partial_pre, "mp", scatter_dimension=0, tiled=True)
        slope = (cotangent.astype(jnp.float32) * gelu_slope(pre) * scale).astype(jnp.bfloat16)
        slope_all = lax.all_gather(slope, "mp", axis=0, tiled=True)
        return backproject(slope_all)

    ascent = weight_grad(w_up)
    squared = lax.psum(jnp.sum(ascent * ascent), ("dp", "mp"))
    size = jnp.sqrt(squared) + 1e-12
    radius = 0.5 * math.sqrt(FF)
    perturbed = (w_up.astype(jnp.float32) + radius * ascent / size).astype(jnp.bfloat16)
    return weight_grad(perturbed)


def solution(mesh):
    placed = (P("dp", "mp"), P("mp"), P("mp", "dp"), P("mp", "dp"))
    return jax.shard_map(
        per_device, mesh=mesh, in_specs=placed, out_specs=P("mp", "dp"), check_vma=False
    )
```

profile of v0, /device:TPU:0, one launch (start us, length us, event | category | flops | bytes accessed | tf_op | source)
XLA Modules:
  0.0 219.0 jit_solution(8525113724424415365)
XLA Ops:
  6.5 0.0 all-gather.2.cloned.1.call-start
  6.5 1.0 convert_reduce_fusion
  7.6 5.8 %all-reduce = (f32[16]{0:T(128)S(1)}, f32[16]{0:T(128)S(1)}) all-reduce(f32[16]{0:T(128)S(1)} %get-tuple-element.6, f32[16]{0:T(128)S(1)} %get-tuple-element.5), channel_id=1, replica_groups=mesh['dp'=16,'mp'=2] {'mp'}, use_global_device_ids=true, to_apply=%region_3.0 | all-reduce | flops 32 | bytes 256 | tf_op jit(solution)/shard_map/psum | solution.py:20
  13.4 1.6 fusion.15
  15.0 0.0 all-gather.2.cloned.1.call-update
  15.1 0.0 copy-start.1
  15.1 0.0 reduce-scatter.3.cloned.1.call-start
  15.1 41.6 %all-gather.2.cloned.1.call-done = bf16[256,3072]{1,0:T(8,128)(2,1)} async-done(((bf16[16,3072]{1,0:T(8,128)(2,1)}), bf16[256,3072]{1,0:T(8,128)(2,1)}) %all-gather.2.cloned.1.call-update) | async-done | bytes 1572880 | tf_op jit(solution)/shard_map/all_gather | solution.py:38
  56.7 8.0 %fusion.18 = f32[256,1536]{1,0:T(8,128)} fusion(bf16[256,3072]{1,0:T(8,128)(2,1)} %all-gather.2.cloned.1.call-done, bf16[3072,1536]{1,0:T(8,128)(2,1)} %param.6), kind=kOutput, calls=%fused_computation.29 | convolution fusion | flops 2415919104 | bytes 12582912 | tf_op jit(solution)/shard_map/dot_general | solution.py:30
  64.7 0.0 reduce-scatter.3.cloned.1.call-update
  64.7 0.0 reduce-scatter.5.cloned.1.call-start
  64.8 25.1 %reduce-scatter.3.cloned.1.call-done = f32[128,1536]{1,0:T(8,128)} async-done(((f32[256,1536]{1,0:T(8,128)}), f32[128,1536]{1,0:T(8,128)}) %reduce-scatter.3.cloned.1.call-update) | async-done | bytes 786448 | tf_op jit(solution)/shard_map/reduce_scatter | solution.py:46
  89.9 0.0 copy-done.1
  89.9 1.5 fusion.2
  91.4 11.5 %all_gather.13 = bf16[256,1536]{1,0:T(8,128)(2,1)S(1)} all-gather(bf16[128,1536]{1,0:T(8,128)(2,1)S(1)} %fusion.2), channel_id=1, replica_groups=mesh['dp'=16,'mp'=2] {'mp'}, dimensions={0}, use_global_device_ids=true | all-gather | bytes 1179648 | tf_op jit(solution)/shard_map/all_gather | solution.py:48
  102.9 0.0 copy-done
  102.9 9.0 %multiply_reduce_fusion = (f32[]{:T(128)}, f32[3072,1536]{1,0:T(8,128)}) fusion(bf16[256,3072]{1,0:T(8,128)(2,1)S(1)} %copy-done, bf16[256,1536]{1,0:T(8,128)(2,1)S(1)} %all_gather.13), kind=kOutput, calls=%fused_computation.1 | convolution fusion | flops 2425356288 | bytes 21233668 | tf_op jit(solution)/shard_map/dot_general | solution.py:37
  111.9 39.6 %psum.23 = f32[]{:T(128)} all-reduce(f32[]{:T(128)} %get-tuple-element.11), channel_id=1, replica_groups=mesh['dp'=16,'mp'=2] {'dp','mp'}, use_global_device_ids=true, to_apply=%region_6.0 | all-reduce | flops 1 | bytes 8 | tf_op jit(solution)/shard_map/psum | solution.py:52
  152.0 12.0 %fusion = f32[256,1536]{1,0:T(8,128)} fusion(bf16[256,3072]{1,0:T(8,128)(2,1)S(1)} %copy-done, f32[3072,1536]{1,0:T(8,128)} %get-tuple-element.12, bf16[3072,1536]{1,0:T(8,128)(2,1)} %param.6, f32[]{:T(128)S(6)} %add.35), kind=kOutput, calls=%fused_computation.2 | convolution fusion | flops 2439512064 | bytes 31457284 | tf_op jit(solution)/shard_map/dot_general | solution.py:30
  164.0 0.0 reduce-scatter.5.cloned.1.call-update
  164.0 27.2 %reduce-scatter.5.cloned.1.call-done = f32[128,1536]{1,0:T(8,128)} async-done(((f32[256,1536]{1,0:T(8,128)}), f32[128,1536]{1,0:T(8,128)}) %reduce-scatter.5.cloned.1.call-update) | async-done | bytes 786448 | tf_op jit(solution)/shard_map/reduce_scatter | solution.py:46
  191.2 1.5 fusion.4
  192.7 11.5 %all_gather.14 = bf16[256,1536]{1,0:T(8,128)(2,1)S(1)} all-gather(bf16[128,1536]{1,0:T(8,128)(2,1)S(1)} %fusion.4), channel_id=1, replica_groups=mesh['dp'=16,'mp'=2] {'mp'}, dimensions={0}, use_global_device_ids=true | all-gather | bytes 1179648 | tf_op jit(solution)/shard_map/all_gather | solution.py:48
  204.2 8.3 %fusion.19 = f32[3072,1536]{1,0:T(8,128)} fusion(bf16[256,3072]{1,0:T(8,128)(2,1)S(1)} %copy-done, bf16[256,1536]{1,0:T(8,128)(2,1)S(1)} %all_gather.14), kind=kOutput, calls=%fused_computation.30 | convolution fusion | flops 2415919104 | bytes 21233664 | tf_op jit(solution)/shard_map/dot_general | solution.py:37
  (2 shorter events, 0.0 us)
Async XLA Ops:
  6.5 50.2 %all-gather.2.cloned.1.call-start = ((), (), s32[]{:S(2)}) async-start(), calls=%async_computation.2 | async-start | bytes 1671168 | tf_op jit(solution)/shard_map/all_gather | solution.py:38
  15.1 74.8 %copy-start.1 = (bf16[128,1536]{1,0:T(8,128)(2,1)S(1)}, bf16[128,1536]{1,0:T(8,128)(2,1)}, u32[]{:S(2)}) copy-start(bf16[128,1536]{1,0:T(8,128)(2,1)} %param.7) | copy-start | bytes 1179652
  15.1 74.8 %reduce-scatter.3.cloned.1.call-start = ((), (), s32[]{:S(2)}) async-start(), calls=%async_computation.3 | async-start | bytes 2359296 | tf_op jit(solution)/shard_map/reduce_scatter | solution.py:46
  56.7 46.2 %copy-start = (bf16[256,3072]{1,0:T(8,128)(2,1)S(1)}, bf16[256,3072]{1,0:T(8,128)(2,1)}, u32[]{:S(2)}) copy-start(bf16[256,3072]{1,0:T(8,128)(2,1)} %all-gather.2.cloned.1.call-done) | copy-start | bytes 4718596
  64.7 126.4 %reduce-scatter.5.cloned.1.call-start = ((), (), s32[]{:S(2)}) async-start(), calls=%async_computation.4 | async-start | bytes 2359296 | tf_op jit(solution)/shard_map/reduce_scatter | solution.py:46
Sparse Core Ops, SparseCore 0:
  15.2 41.4 all-gather.1
  64.9 24.9 reduce-scatter.2
  164.1 26.9 reduce-scatter.4
where the time goes:
time: 219 us
  waiting for transfers between devices  93.8 us (43%)
  blocking collectives  68.5 us (31%)
  matrix products  37.2 us (17%)
  between operations  13.7 us (6%)
  other arithmetic  5.69 us (3%)
    reduce_scatter x2, waiting for transfers between devices, weight_grad(): pre = lax.psum_scatter(partial_pre, 'mp', scatter_dimension=0, tiled=True)  52.2 us
    all_gather x1, waiting for transfers between devices, backproject(): lax.all_gather(normed, 'dp', axis=0, tiled=True)  41.6 us
    psum x1, blocking collectives, per_device(): squared = lax.psum(jnp.sum(ascent * ascent), ('dp', 'mp'))  39.6 us
    all_gather x2, blocking collectives, weight_grad(): slope_all = lax.all_gather(slope, 'mp', axis=0, tiled=True)  23.1 us
    dot_general x2, matrix products, project(): jnp.dot(lax.all_gather(normed, 'dp', axis=0, tiled=True), weights, prefer...  20 us
    dot_general x2, matrix products, backproject(): lax.dot_general(lax.all_gather(normed, 'dp', axis=0, tiled=True), slope_a...  17.3 us
    psum x1, blocking collectives, per_device(): lax.psum((jnp.sum(values, axis=1), jnp.sum(values * values, axis=1)), 'mp')  5.84 us
  transfers between devices with their start and end apart: 3, of which 3 were waited for; matrix products, arithmetic and copies ran while one was open for 0% of the time, Pallas kernels for 0%

commit v1 on v0

v1 whole, which is shorter than its diff:
```python
import functools
import math

import jax
import jax.numpy as jnp
from jax import lax
from jax.experimental import pallas as pl
from jax.experimental.pallas import tpu as pltpu
from jax.sharding import PartitionSpec as P

FF = 24576
MESH = pl.DeviceIdType.MESH
F32 = jnp.float32
BF16 = jnp.bfloat16


def gelu_slope(value):
    cdf = 0.5 * (1.0 + lax.erf(value * (1.0 / math.sqrt(2.0))))
    dens = jnp.exp(-0.5 * value * value) * (1.0 / math.sqrt(2.0 * math.pi))
    return cdf + value * dens


def remote(src, dst, send_sem, recv_sem, device):
    return pltpu.make_async_remote_copy(
        src_ref=src, dst_ref=dst, send_sem=send_sem, recv_sem=recv_sem,
        device_id=device, device_id_type=MESH,
    )


def slopes_kernel(
    cfg,
    tok_ref, gain_ref, w_hbm, cot_hbm,
    nt_ref, pre_ref, gs_ref, cot_ref, norm_ref,
    xs, nall, w, st_part, st_part_in, st_all, own, sendb, recvb,
    g_part, g_part_in, g_all, slope, nb,
    w_sem, c_sem, z_ss, y_ss, core_ss, x_rs,
    stp_ss, stp_rs, st_ss, st_rs, cot_ss, cot_rs, pre_ss, pre_rs,
    gp_ss, gp_rs, g_ss, g_rs, nb_ss, nb_rs,
):
    n, m, lines, width_all, token_count = cfg
    rows, depth = tok_ref.shape
    cot_rows, cols = cot_hbm.shape
    chunks, _, chunk = own.shape
    cores = 2
    per_line = n // (lines * cores)
    scale = 1.0 / math.sqrt(token_count)
    me = lax.axis_index("dp")
    my_mp = lax.axis_index("mp")
    core = lax.rem(me, cores)
    across = lax.rem(me // cores, per_line)
    along = me // (cores * per_line)

    def index(a, b, c):
        return (a * per_line + b) * cores + c

    def dp_peer(k):
        return lax.rem(me + k, n)

    def mp_peer(k):
        return lax.rem(my_mp + k, m)

    w_copy = pltpu.make_async_copy(w_hbm, w, w_sem)
    w_copy.start()
    cot_dst = cot_ref.at[pl.ds(pl.multiple_of(my_mp * cot_rows, cot_rows), cot_rows)]
    cot_copy = pltpu.make_async_copy(cot_hbm, cot_dst, c_sem)
    cot_copy.start()

    barrier = pltpu.get_barrier_semaphore()

    @pl.loop(1, n)
    def _(k):
        pl.semaphore_signal(barrier, inc=1, device_id={"dp": dp_peer(k)}, device_id_type=MESH)

    @pl.loop(1, m)
    def _(k):
        pl.semaphore_signal(barrier, inc=1, device_id={"mp": mp_peer(k)}, device_id_type=MESH)

    values = tok_ref[...].astype(F32)
    lane = lax.broadcasted_iota(jnp.int32, (rows, 128), 1)
    sums = jnp.sum(values, axis=1, keepdims=True)
    squares = jnp.sum(values * values, axis=1, keepdims=True)
    st_part[...] = jnp.where(lane == 0, sums, squares)
    xs[me] = tok_ref[...]

    pl.semaphore_wait(barrier, n + m - 2)

    def line_copy(k):
        return remote(tok_ref, xs.at[me], z_ss.at[k], x_rs.at[me],
                      {"dp": index(lax.rem(along + k, lines), across, core)})

    def across_copy(k, j):
        src = index(lax.rem(along + k, lines), across, core)
        to = index(along, lax.rem(across + j, per_line), core)
        return remote(xs.at[src], xs.at[src], y_ss.at[k, j], x_rs.at[src], {"dp": to})

    def core_copy(k, j):
        src = index(lax.rem(along + k, lines), lax.rem(across + j, per_line), core)
        return remote(xs.at[src], xs.at[src], core_ss.at[k, j], x_rs.at[src],
                      {"dp": index(along, across, 1 - core)})

    def arrived(src):
        remote(xs.at[src], xs.at[src], z_ss.at[0], x_rs.at[src], {"dp": dp_peer(1)}).wait_recv()

    def stp_copy(k):
        return remote(st_part, st_part_in.at[my_mp], stp_ss.at[k], stp_rs.at[my_mp],
                      {"mp": mp_peer(k)})

    def cot_send(k):
        return remote(cot_hbm, cot_dst, cot_ss.at[k], cot_rs.at[my_mp], {"mp": mp_peer(k)})

    for k in range(1, m):
        stp_copy(k).start()
    for k in range(1, lines):
        line_copy(k).start()
    for j in range(1, per_line):
        across_copy(0, j).start()
    core_copy(0, 0).start()

    total = st_part[...]
    for k in range(1, m):
        p = mp_peer(k)
        remote(st_part, st_part_in.at[p], stp_ss.at[0], stp_rs.at[p], {"mp": p}).wait_recv()
        total = total + st_part_in[p]
    for k in range(1, m):
        cot_send(k).start()
    mean = total[:, 0:1] / width_all
    var = total[:, 1:2] / width_all - mean * mean
    st_all[me] = jnp.where(lane == 0, mean, lax.rsqrt(var + 1e-06))

    def st_copy(k):
        return remote(st_all.at[me], st_all.at[me], st_ss.at[k], st_rs.at[me],
                      {"dp": dp_peer(k)})

    @pl.loop(1, n)
    def _(k):
        st_copy(k).start()

    for k in range(1, lines):
        arrived(index(lax.rem(along + k, lines), across, core))
        for j in range(1, per_line):
            across_copy(k, j).start()
        core_copy(k, 0).start()

    @pl.loop(1, n)
    def _(k):
        p = dp_peer(k)
        remote(st_all.at[p], st_all.at[p], st_ss.at[0], st_rs.at[p], {"dp": p}).wait_recv()

    def normalize(src):
        x = xs[src].astype(F32)
        st = st_all[src]
        value = (x - st[:, 0:1]) * st[:, 1:2] * gain_ref[...]
        nall[pl.ds(pl.multiple_of(src * rows, rows), rows), :] = value.astype(BF16)

    @pl.loop(0, lines)
    def _(k):
        normalize(index(lax.rem(along + k, lines), across, core))

    for k in range(lines):
        for j in range(1, per_line):
            arrived(index(lax.rem(along + k, lines), lax.rem(across + j, per_line), core))
            core_copy(k, j).start()

    @pl.loop(0, lines * (per_line - 1))
    def _(i):
        k = i // (per_line - 1)
        j = 1 + lax.rem(i, per_line - 1)
        normalize(index(lax.rem(along + k, lines), lax.rem(across + j, per_line), core))

    @pl.loop(0, lines * per_line)
    def _(i):
        k = i // per_line
        j = lax.rem(i, per_line)
        src = index(lax.rem(along + k, lines), lax.rem(across + j, per_line), 1 - core)
        arrived(src)
        normalize(src)

    w_copy.wait()

    def pre_copy(i, k):
        return remote(sendb.at[i], recvb.at[my_mp, i], pre_ss.at[i, k], pre_rs.at[my_mp, i],
                      {"mp": mp_peer(k)})

    @pl.loop(0, chunks)
    def _(i):
        off = pl.multiple_of(i * chunk, chunk)
        part = jnp.dot(nall[...], w[:, pl.ds(off, chunk)], preferred_element_type=F32)
        own[i] = part
        sendb[i] = part.astype(BF16)
        for k in range(1, m):
            pre_copy(i, k).start()

    mine = pl.ds(pl.multiple_of(me * rows, rows), rows)
    g_part[...] = lax.dot_general(
        nall[mine, :], nall[...], (((1,), (1,)), ((), ())), preferred_element_type=F32
    )

    def gp_copy(k):
        return remote(g_part, g_part_in.at[my_mp], gp_ss.at[k], gp_rs.at[my_mp],
                      {"mp": mp_peer(k)})

    def g_copy(k):
        return remote(g_all.at[mine], g_all.at[mine], g_ss.at[k], g_rs.at[me],
                      {"dp": dp_peer(k)})

    for k in range(1, m):
        gp_copy(k).start()

    @pl.loop(0, depth // 256)
    def _(i):
        off = pl.multiple_of(i * 256, 256)
        nt_ref[pl.ds(off, 256), :] = nall[:, pl.ds(off, 256)].T

    gram = g_part[...]
    for k in range(1, m):
        p = mp_peer(k)
        remote(g_part, g_part_in.at[p], gp_ss.at[0], gp_rs.at[p], {"mp": p}).wait_recv()
        gram = gram + g_part_in[p]
    g_all[mine, :] = gram

    @pl.loop(1, n)
    def _(k):
        g_copy(k).start()

    cot_copy.wait()
    for k in range(1, m):
        p = mp_peer(k)
        dst = cot_ref.at[pl.ds(pl.multiple_of(p * cot_rows, cot_rows), cot_rows)]
        remote(cot_hbm, dst, cot_ss.at[0], cot_rs.at[p], {"mp": p}).wait_recv()

    @pl.loop(1, n)
    def _(k):
        p = dp_peer(k)
        dst = g_all.at[pl.ds(pl.multiple_of(p * rows, rows), rows)]
        remote(dst, dst, g_ss.at[0], g_rs.at[p], {"dp": p}).wait_recv()

    nb[me] = jnp.zeros_like(nb[me])

    @pl.loop(0, chunks)
    def _(i):
        off = pl.multiple_of(i * chunk, chunk)
        pre = own[i]
        for k in range(1, m):
            p = mp_peer(k)
            remote(sendb.at[i], recvb.at[p, i], pre_ss.at[i, 0], pre_rs.at[p, i],
                   {"mp": p}).wait_recv()
            pre = pre + recvb[p, i].astype(F32)
        pre_ref[:, pl.ds(off, chunk)] = pre
        cot = cot_ref[:, pl.ds(off, chunk)].astype(F32)
        slope[...] = (cot * gelu_slope(pre) * scale).astype(BF16)
        gram = g_all[...]
        high = gram.astype(BF16)
        rest = gram - high.astype(F32)
        mid = rest.astype(BF16)
        low = (rest - mid.astype(F32)).astype(BF16)
        s = slope[...]
        gs = (
            jnp.dot(low, s, preferred_element_type=F32)
            + jnp.dot(mid, s, preferred_element_type=F32)
            + jnp.dot(high, s, preferred_element_type=F32)
        )
        gs_ref[:, pl.ds(off, chunk)] = gs
        nb[me] += jnp.full((8, 128), jnp.sum(gs * s.astype(F32)), F32)

    def nb_copy(k):
        return remote(nb.at[me], nb.at[me], nb_ss.at[k], nb_rs.at[me], {"dp": dp_peer(k)})

    @pl.loop(1, n)
    def _(k):
        nb_copy(k).start()

    @pl.loop(1, n)
    def _(k):
        st_copy(k).wait_send()
        g_copy(k).wait_send()

    for k in range(1, lines):
        line_copy(k).wait_send()
    for k in range(lines):
        for j in range(per_line):
            core_copy(k, j).wait_send()
            if j > 0:
                across_copy(k, j).wait_send()
    for k in range(1, m):
        stp_copy(k).wait_send()
        cot_send(k).wait_send()
        gp_copy(k).wait_send()

        @pl.loop(0, chunks)
        def _(i):
            pre_copy(i, k).wait_send()

    @pl.loop(1, n)
    def _(k):
        p = dp_peer(k)
        remote(nb.at[p], nb.at[p], nb_ss.at[0], nb_rs.at[p], {"dp": p}).wait_recv()
        nb_copy(k).wait_send()

    norm_ref[...] = jnp.sum(nb[...], axis=0)


def grad_kernel(token_count, norm_ref, nt_ref, pre_ref, gs_ref, cot_ref, out_ref):
    scale = 1.0 / math.sqrt(token_count)
    size = jnp.sqrt(jnp.maximum(norm_ref[0:1, 0:1], 0.0)) + 1e-12
    radius = 0.5 * math.sqrt(FF)
    pre = pre_ref[...] + radius * gs_ref[...] / size
    slope = (cot_ref[...].astype(F32) * gelu_slope(pre) * scale).astype(BF16)
    out_ref[...] = jnp.dot(nt_ref[...], slope, preferred_element_type=F32)


def per_device(tokens, norm_gain, w_up, cotangent):
    n, m = lax.axis_size("dp"), lax.axis_size("mp")
    rows, depth = tokens.shape
    count = rows * n
    cols = w_up.shape[1]
    lines = 4
    chunk = 256 if cols % 256 == 0 else 128
    chunks = cols // chunk
    per_line = n // (2 * lines)
    cot_rows = cotangent.shape[0]
    dma, vmem = pltpu.SemaphoreType.DMA, pltpu.VMEM
    whole = pl.BlockSpec(memory_space=pltpu.VMEM)
    hbm = pl.BlockSpec(memory_space=pl.ANY)
    cfg = (n, m, lines, depth * m, count)
    nt, pre, gs, cot, norm = pl.pallas_call(
        functools.partial(slopes_kernel, cfg),
        out_shape=(
            jax.ShapeDtypeStruct((depth, count), BF16),
            jax.ShapeDtypeStruct((count, cols), F32),
            jax.ShapeDtypeStruct((count, cols), F32),
            jax.ShapeDtypeStruct((count, cols), BF16),
            jax.ShapeDtypeStruct((8, 128), F32),
        ),
        in_specs=[whole, whole, hbm, hbm],
        out_specs=[whole] * 5,
        scratch_shapes=[
            vmem((n, rows, depth), BF16),
            vmem((count, depth), BF16),
            vmem((depth, cols), BF16),
            vmem((rows, 128), F32),
            vmem((m, rows, 128), F32),
            vmem((n, rows, 128), F32),
            vmem((chunks, count, chunk), F32),
            vmem((chunks, count, chunk), BF16),
            vmem((m, chunks, count, chunk), BF16),
            vmem((rows, count), F32),
            vmem((m, rows, count), F32),
            vmem((count, count), F32),
            vmem((count, chunk), BF16),
            vmem((n, 8, 128), F32),
            dma(()), dma(()), dma((lines,)), dma((lines, per_line)), dma((lines, per_line)),
            dma((n,)),
            dma((m,)), dma((m,)), dma((n,)), dma((n,)), dma((m,)), dma((m,)),
            dma((chunks, m)), dma((m, chunks)),
            dma((m,)), dma((m,)), dma((n,)), dma((n,)), dma((n,)), dma((n,)),
        ],
        compiler_params=pltpu.CompilerParams(
            collective_id=0, has_side_effects=True, vmem_limit_bytes=56 * 2**20
        ),
        name="slopes",
    )(tokens, norm_gain.reshape(1, depth), w_up, cotangent)

    return pl.pallas_call(
        functools.partial(grad_kernel, count),
        grid=(chunks,),
        out_shape=jax.ShapeDtypeStruct((depth, cols), F32),
        in_specs=[
            pl.BlockSpec((8, 128), lambda i: (0, 0)),
            pl.BlockSpec((depth, count), lambda i: (0, 0)),
            pl.BlockSpec((count, chunk), lambda i: (0, i)),
            pl.BlockSpec((count, chunk), lambda i: (0, i)),
            pl.BlockSpec((count, chunk), lambda i: (0, i)),
        ],
        out_specs=pl.BlockSpec((depth, chunk), lambda i: (0, i)),
        compiler_params=pltpu.CompilerParams(vmem_limit_bytes=40 * 2**20),
        name="grad",
    )(norm, nt, pre, gs, cot)


def solution(mesh):
    placed = (P("dp", "mp"), P("mp"), P("mp", "dp"), P("mp", "dp"))
    return jax.shard_map(
        per_device, mesh=mesh, in_specs=placed, out_specs=P("mp", "dp"), check_vma=False
    )
```

time: 219 us -> 78.8 us (0.36)
  waiting for transfers between devices: 93.8 us -> 0 us
  Pallas kernels: 0 us -> 72.5 us
  blocking collectives: 68.5 us -> 0 us
  matrix products: 37.2 us -> 0 us
  between operations: 13.7 us -> 0.02 us
  local copies, waits for them, and re-layouts: 0.01 us -> 6.03 us
  other arithmetic: 5.69 us -> 0 us
    pallas_call x0 -> x2, Pallas kernels: none -> 72.5 us  [the longest x1 64.1 us: per_device(): pl.pallas_call(functools.partial(slopes_kernel, cfg), out_shape=(jax.Shap...]
    reduce_scatter x2 -> x0, waiting for transfers between devices: 52.2 us -> none  [weight_grad(): pre = lax.psum_scatter(partial_pre, 'mp', scatter_dimension=0, tiled=True)]
    psum x2 -> x0, blocking collectives: 45.4 us -> none  [the longest x1 39.6 us: per_device(): squared = lax.psum(jnp.sum(ascent * ascent), ('dp', 'mp'))]
    all_gather x1 -> x0, waiting for transfers between devices: 41.6 us -> none  [backproject(): lax.all_gather(normed, 'dp', axis=0, tiled=True)]
    dot_general x4 -> x0, matrix products: 37.2 us -> none  [the longest x2 20 us: project(): jnp.dot(lax.all_gather(normed, 'dp', axis=0, tiled=True), weights, prefer...]
    all_gather x2 -> x0, blocking collectives: 23.1 us -> none  [weight_grad(): slope_all = lax.all_gather(slope, 'mp', axis=0, tiled=True)]
    unnamed x4 -> x10, local copies, waits for them, and re-layouts: 0.01 us -> 6.03 us
    convert_element_type x3 -> x0, other arithmetic: 4.65 us -> none  [the longest x2 3.01 us: weight_grad(): (cotangent.astype(jnp.float32) * gelu_slope(pre) * scale).astype(jnp.bflo...]
  transfers between devices with their start and end apart: 3 -> 0, of which waited for: 3 -> 0; matrix products, arithmetic and copies ran while one was open for 0% -> 0% of each run, Pallas kernels for 0% -> 0%
where the time goes in v1:
time: 78.8 us; the launch traced here: 78.5 us
  Pallas kernels  72.5 us (92%)
  local copies, waits for them, and re-layouts  6.03 us (8%)
    pallas_call x1, Pallas kernels, per_device(): pl.pallas_call(functools.partial(slopes_kernel, cfg), out_shape=(jax.Shap...  64.1 us
    pallas_call x1, Pallas kernels, per_device(): pl.pallas_call(functools.partial(grad_kernel, count), grid=(chunks,), out...  8.4 us
    unnamed x10, local copies, waits for them, and re-layouts  6.03 us

profile of v1, /device:TPU:0, one launch (start us, length us, event | category | flops | bytes accessed | tf_op | source)
XLA Modules:
  0.0 78.5 jit_solution(926077588734846087)
XLA Ops:
  0.0 64.1 %slopes.1 = (bf16[3072,256]{1,0:T(8,128)(2,1)}, f32[256,1536]{1,0:T(8,128)}, f32[256,1536]{1,0:T(8,128)}, bf16[256,1536]{1,0:T(8,128)(2,1)}, f32[8,128]{1,0:T(8,128)}) custom-call(bf16[16,3072]{1,0:T(8,128)(2,1)} %tok_ref.1, f32[1,3072]{1,0:T(1,128)} %bitcast.1, bf16[3072,1536]{1,0:T(8,128)(2,1)} %w_hbm.1, bf16[128,1536]{1,0:T(8,128)(2,1)} %cot_hbm.1), custom_call_target="tpu_custom_call" | custom-call | tf_op jit(solution)/shard_map/slopes/pallas_call | solution.py:325
  64.1 0.0 copy-start
  64.1 1.4 %copy-done = bf16[3072,256]{1,0:T(8,128)(2,1)S(1)} copy-done((bf16[3072,256]{1,0:T(8,128)(2,1)S(1)}, bf16[3072,256]{1,0:T(8,128)(2,1)}, u32[]{:S(2)}) %copy-start) | copy-done | bytes 1572888
  65.5 0.0 copy-start.1
  65.5 1.4 %copy-done.1 = f32[256,1536]{1,0:T(8,128)S(1)} copy-done((f32[256,1536]{1,0:T(8,128)S(1)}, f32[256,1536]{1,0:T(8,128)}, u32[]{:S(2)}) %copy-start.1) | copy-done | bytes 1572888
  66.9 0.0 copy-start.2
  66.9 1.4 %copy-done.2 = f32[256,1536]{1,0:T(8,128)S(1)} copy-done((f32[256,1536]{1,0:T(8,128)S(1)}, f32[256,1536]{1,0:T(8,128)}, u32[]{:S(2)}) %copy-start.2) | copy-done | bytes 1572888
  68.3 0.0 copy-start.3
  68.3 1.1 %copy-done.3 = bf16[256,1536]{1,0:T(8,128)(2,1)S(1)} copy-done((bf16[256,1536]{1,0:T(8,128)(2,1)S(1)}, bf16[256,1536]{1,0:T(8,128)(2,1)}, u32[]{:S(2)}) %copy-start.3) | copy-done | bytes 786456
  69.4 0.0 copy-start.4
  69.4 0.7 copy-done.4
  70.1 8.4 %grad.1 = f32[3072,1536]{1,0:T(8,128)} custom-call(f32[8,128]{1,0:T(8,128)S(1)} %copy-done.4, bf16[3072,256]{1,0:T(8,128)(2,1)S(1)} %copy-done, f32[256,1536]{1,0:T(8,128)S(1)} %copy-done.1, f32[256,1536]{1,0:T(8,128)S(1)} %copy-done.2, bf16[256,1536]{1,0:T(8,128)(2,1)S(1)} %copy-done.3), custom_call_target="tpu_custom_call" | custom-call | tf_op jit(solution)/shard_map/grad/pallas_call | solution.py:363
Async XLA Ops:
  64.1 1.4 %copy-start = (bf16[3072,256]{1,0:T(8,128)(2,1)S(1)}, bf16[3072,256]{1,0:T(8,128)(2,1)}, u32[]{:S(2)}) copy-start(bf16[3072,256]{1,0:T(8,128)(2,1)} %get-tuple-element.11.nt_ref) | copy-start | bytes 4718596
  65.5 1.4 %copy-start.1 = (f32[256,1536]{1,0:T(8,128)S(1)}, f32[256,1536]{1,0:T(8,128)}, u32[]{:S(2)}) copy-start(f32[256,1536]{1,0:T(8,128)} %get-tuple-element.12.pre_ref) | copy-start | bytes 4718596
  66.9 1.4 %copy-start.2 = (f32[256,1536]{1,0:T(8,128)S(1)}, f32[256,1536]{1,0:T(8,128)}, u32[]{:S(2)}) copy-start(f32[256,1536]{1,0:T(8,128)} %get-tuple-element.13.gs_ref) | copy-start | bytes 4718596
  68.3 1.1 %copy-start.3 = (bf16[256,1536]{1,0:T(8,128)(2,1)S(1)}, bf16[256,1536]{1,0:T(8,128)(2,1)}, u32[]{:S(2)}) copy-start(bf16[256,1536]{1,0:T(8,128)(2,1)} %get-tuple-element.14.cot_ref) | copy-start | bytes 2359300
  69.4 0.7 copy-start.4

commit v2 on v1

--- a/solution.py
+++ b/solution.py
@@ -30,10 +30,11 @@
 def slopes_kernel(
     cfg,
     tok_ref, gain_ref, w_hbm, cot_hbm,
-    nt_ref, pre_ref, gs_ref, cot_ref, norm_ref,
+    nt_hbm, pre_hbm, gs_hbm, cot_out, norm_ref,
+    nt_ref, pre_ref, gs_ref, cot_ref, g_terms,
     xs, nall, w, st_part, st_part_in, st_all, own, sendb, recvb,
     g_part, g_part_in, g_all, slope, nb,
-    w_sem, c_sem, z_ss, y_ss, core_ss, x_rs,
+    w_sem, c_sem, o_sem, pre_os, gs_os, z_ss, y_ss, core_ss, x_rs,
     stp_ss, stp_rs, st_ss, st_rs, cot_ss, cot_rs, pre_ss, pre_rs,
     gp_ss, gp_rs, g_ss, g_rs, nb_ss, nb_rs,
 ):
@@ -84,22 +85,36 @@
 
     pl.semaphore_wait(barrier, n + m - 2)
 
-    def line_copy(k):
-        return remote(tok_ref, xs.at[me], z_ss.at[k], x_rs.at[me],
-                      {"dp": index(lax.rem(along + k, lines), across, core)})
-
-    def across_copy(k, j):
-        src = index(lax.rem(along + k, lines), across, core)
+    def line_copy(src_a, up):
+        src = index(src_a, across, core)
+        to = index(along + 1 if up else along - 1, across, core)
+        return remote(xs.at[src], xs.at[src], z_ss.at[int(up), src_a], x_rs.at[src], {"dp": to})
+
+    def across_copy(src_a, j):
+        src = index(src_a, across, core)
         to = index(along, lax.rem(across + j, per_line), core)
-        return remote(xs.at[src], xs.at[src], y_ss.at[k, j], x_rs.at[src], {"dp": to})
-
-    def core_copy(k, j):
-        src = index(lax.rem(along + k, lines), lax.rem(across + j, per_line), core)
-        return remote(xs.at[src], xs.at[src], core_ss.at[k, j], x_rs.at[src],
+        return remote(xs.at[src], xs.at[src], y_ss.at[src_a, j], x_rs.at[src], {"dp": to})
+
+    def core_copy(src_a, j):
+        src = index(src_a, lax.rem(across + j, per_line), core)
+        return remote(xs.at[src], xs.at[src], core_ss.at[src_a, j], x_rs.at[src],
                       {"dp": index(along, across, 1 - core)})
 
     def arrived(src):
-        remote(xs.at[src], xs.at[src], z_ss.at[0], x_rs.at[src], {"dp": dp_peer(1)}).wait_recv()
+        remote(xs.at[src], xs.at[src], z_ss.at[0, 0], x_rs.at[src], {"dp": dp_peer(1)}).wait_recv()
+
+    by_distance = [(along - s if low else along + s, low) for s in range(1, lines) for low in (True, False)]
+
+    def there(pos, low):
+        return pos >= 0 if low else pos < lines
+
+    def can_go(up):
+        return along + 1 < lines if up else along > 0
+
+    def across_step(pos):
+        for j in range(1, per_line):
+            arrived(index(pos, lax.rem(across + j, per_line), core))
+            core_copy(pos, j).start()
 
     def stp_copy(k):
         return remote(st_part, st_part_in.at[my_mp], stp_ss.at[k], stp_rs.at[my_mp],
@@ -110,11 +125,13 @@
 
     for k in range(1, m):
         stp_copy(k).start()
-    for k in range(1, lines):
-        line_copy(k).start()
+    for up in (True, False):
+        @pl.when(can_go(up))
+        def _():
+            line_copy(along, up).start()
     for j in range(1, per_line):
-        across_copy(0, j).start()
-    core_copy(0, 0).start()
+        across_copy(along, j).start()
+    core_copy(along, 0).start()
 
     total = st_part[...]
     for k in range(1, m):
@@ -135,11 +152,18 @@
     def _(k):
         st_copy(k).start()
 
-    for k in range(1, lines):
-        arrived(index(lax.rem(along + k, lines), across, core))
-        for j in range(1, per_line):
-            across_copy(k, j).start()
-        core_copy(k, 0).start()
+    for pos, low in by_distance:
+        @pl.when(there(pos, low))
+        def _():
+            arrived(index(pos, across, core))
+
+            @pl.when(can_go(low))
+            def _():
+                line_copy(pos, low).start()
+
+            for j in range(1, per_line):
+                across_copy(pos, j).start()
+            core_copy(pos, 0).start()
 
     @pl.loop(1, n)
     def _(k):
@@ -156,10 +180,11 @@
     def _(k):
         normalize(index(lax.rem(along + k, lines), across, core))
 
-    for k in range(lines):
-        for j in range(1, per_line):
-            arrived(index(lax.rem(along + k, lines), lax.rem(across + j, per_line), core))
-            core_copy(k, j).start()
+    across_step(along)
+    for pos, low in by_distance:
+        @pl.when(there(pos, low))
+        def _():
+            across_step(pos)
 
     @pl.loop(0, lines * (per_line - 1))
     def _(i):
@@ -181,8 +206,7 @@
         return remote(sendb.at[i], recvb.at[my_mp, i], pre_ss.at[i, k], pre_rs.at[my_mp, i],
                       {"mp": mp_peer(k)})
 
-    @pl.loop(0, chunks)
-    def _(i):
+    def project(i):
         off = pl.multiple_of(i * chunk, chunk)
         part = jnp.dot(nall[...], w[:, pl.ds(off, chunk)], preferred_element_type=F32)
         own[i] = part
@@ -190,6 +214,8 @@
         for k in range(1, m):
             pre_copy(i, k).start()
 
+    project(0)
+
     mine = pl.ds(pl.multiple_of(me * rows, rows), rows)
     g_part[...] = lax.dot_general(
         nall[mine, :], nall[...], (((1,), (1,)), ((), ())), preferred_element_type=F32
@@ -206,10 +232,9 @@
     for k in range(1, m):
         gp_copy(k).start()
 
-    @pl.loop(0, depth // 256)
-    def _(i):
-        off = pl.multiple_of(i * 256, 256)
-        nt_ref[pl.ds(off, 256), :] = nall[:, pl.ds(off, 256)].T
+    @pl.loop(1, chunks)
+    def _(i):
+        project(i)
 
     gram = g_part[...]
     for k in range(1, m):
@@ -222,6 +247,14 @@
     def _(k):
         g_copy(k).start()
 
+    @pl.loop(0, depth // 256)
+    def _(i):
+        off = pl.multiple_of(i * 256, 256)
+        nt_ref[pl.ds(off, 256), :] = nall[:, pl.ds(off, 256)].T
+
+    nt_copy = pltpu.make_async_copy(nt_ref, nt_hbm, o_sem.at[0])
+    nt_copy.start()
+
     cot_copy.wait()
     for k in range(1, m):
         p = mp_peer(k)
@@ -233,6 +266,18 @@
         p = dp_peer(k)
         dst = g_all.at[pl.ds(pl.multiple_of(p * rows, rows), rows)]
         remote(dst, dst, g_ss.at[0], g_rs.at[p], {"dp": p}).wait_recv()
+
+    cot_write = pltpu.make_async_copy(cot_ref, cot_out, o_sem.at[1])
+    cot_write.start()
+
+    rest = g_all[...]
+    for t in range(3):
+        g_terms[t] = rest.astype(BF16)
+        rest = rest - g_terms[t].astype(F32)
+
+    def out_copy(i, buf, dst, sem):
+        cut = pl.ds(pl.multiple_of(i * chunk, chunk), chunk)
+        return pltpu.make_async_copy(buf.at[:, cut], dst.at[:, cut], sem.at[i])
 
     nb[me] = jnp.zeros_like(nb[me])
 
@@ -248,18 +293,15 @@
         pre_ref[:, pl.ds(off, chunk)] = pre
         cot = cot_ref[:, pl.ds(off, chunk)].astype(F32)
         slope[...] = (cot * gelu_slope(pre) * scale).astype(BF16)
-        gram = g_all[...]
-        high = gram.astype(BF16)
-        rest = gram - high.astype(F32)
-        mid = rest.astype(BF16)
-        low = (rest - mid.astype(F32)).astype(BF16)
+        out_copy(i, pre_ref, pre_hbm, pre_os).start()
         s = slope[...]
         gs = (
-            jnp.dot(low, s, preferred_element_type=F32)
-            + jnp.dot(mid, s, preferred_element_type=F32)
-            + jnp.dot(high, s, preferred_element_type=F32)
+            jnp.dot(g_terms[2], s, preferred_element_type=F32)
+            + jnp.dot(g_terms[1], s, preferred_element_type=F32)
+            + jnp.dot(g_terms[0], s, preferred_element_type=F32)
         )
         gs_ref[:, pl.ds(off, chunk)] = gs
+        out_copy(i, gs_ref, gs_hbm, gs_os).start()
         nb[me] += jnp.full((8, 128), jnp.sum(gs * s.astype(F32)), F32)
 
     def nb_copy(k):
@@ -274,13 +316,26 @@
         st_copy(k).wait_send()
         g_copy(k).wait_send()
 
-    for k in range(1, lines):
-        line_copy(k).wait_send()
-    for k in range(lines):
+    for pos, low in [(along, True), (along, False)] + by_distance:
+        @pl.when(jnp.logical_and(there(pos, low), can_go(low)))
+        def _():
+            line_copy(pos, low).wait_send()
+
+    @pl.loop(0, lines)
+    def _(pos):
         for j in range(per_line):
-            core_copy(k, j).wait_send()
+            core_copy(pos, j).wait_send()
             if j > 0:
-                across_copy(k, j).wait_send()
+                across_copy(pos, j).wait_send()
+
+    nt_copy.wait()
+    cot_write.wait()
+
+    @pl.loop(0, chunks)
+    def _(i):
+        out_copy(i, pre_ref, pre_hbm, pre_os).wait()
+        out_copy(i, gs_ref, gs_hbm, gs_os).wait()
+
     for k in range(1, m):
         stp_copy(k).wait_send()
         cot_send(k).wait_send()
@@ -299,13 +354,18 @@
     norm_ref[...] = jnp.sum(nb[...], axis=0)
 
 
-def grad_kernel(token_count, norm_ref, nt_ref, pre_ref, gs_ref, cot_ref, out_ref):
+def grad_kernel(token_count, norm_ref, nt_ref, pre_ref, gs_ref, cot_ref, out_ref, slope_ref):
+    @pl.when(pl.program_id(0) == 0)
+    def _():
+        slope_ref[...] = jnp.zeros_like(slope_ref)
+
+    before = slope_ref[...]
     scale = 1.0 / math.sqrt(token_count)
     size = jnp.sqrt(jnp.maximum(norm_ref[0:1, 0:1], 0.0)) + 1e-12
     radius = 0.5 * math.sqrt(FF)
     pre = pre_ref[...] + radius * gs_ref[...] / size
-    slope = (cot_ref[...].astype(F32) * gelu_slope(pre) * scale).astype(BF16)
-    out_ref[...] = jnp.dot(nt_ref[...], slope, preferred_element_type=F32)
+    out_ref[...] = jnp.dot(nt_ref[...], before, preferred_element_type=F32)
+    slope_ref[...] = (cot_ref[...].astype(F32) * gelu_slope(pre) * scale).astype(BF16)
 
 
 def per_device(tokens, norm_gain, w_up, cotangent):
@@ -332,8 +392,13 @@
             jax.ShapeDtypeStruct((8, 128), F32),
         ),
         in_specs=[whole, whole, hbm, hbm],
-        out_specs=[whole] * 5,
+        out_specs=[hbm] * 4 + [whole],
         scratch_shapes=[
+            vmem((depth, count), BF16),
+            vmem((count, cols), F32),
+            vmem((count, cols), F32),
+            vmem((count, cols), BF16),
+            vmem((3, count, count), BF16),
             vmem((n, rows, depth), BF16),
             vmem((count, depth), BF16),
             vmem((depth, cols), BF16),
@@ -348,7 +413,8 @@
             vmem((count, count), F32),
             vmem((count, chunk), BF16),
             vmem((n, 8, 128), F32),
-            dma(()), dma(()), dma((lines,)), dma((lines, per_line)), dma((lines, per_line)),
+            dma(()), dma(()), dma((2,)), dma((chunks,)), dma((chunks,)),
+            dma((2, lines)), dma((lines, per_line)), dma((lines, per_line)),
             dma((n,)),
             dma((m,)), dma((m,)), dma((n,)), dma((n,)), dma((m,)), dma((m,)),
             dma((chunks, m)), dma((m, chunks)),
@@ -362,17 +428,18 @@
 
     return pl.pallas_call(
         functools.partial(grad_kernel, count),
-        grid=(chunks,),
+        grid=(chunks + 1,),
         out_shape=jax.ShapeDtypeStruct((depth, cols), F32),
         in_specs=[
             pl.BlockSpec((8, 128), lambda i: (0, 0)),
             pl.BlockSpec((depth, count), lambda i: (0, 0)),
-            pl.BlockSpec((count, chunk), lambda i: (0, i)),
-            pl.BlockSpec((count, chunk), lambda i: (0, i)),
-            pl.BlockSpec((count, chunk), lambda i: (0, i)),
+            pl.BlockSpec((count, chunk), lambda i: (0, jnp.minimum(i, chunks - 1))),
+            pl.BlockSpec((count, chunk), lambda i: (0, jnp.minimum(i, chunks - 1))),
+            pl.BlockSpec((count, chunk), lambda i: (0, jnp.minimum(i, chunks - 1))),
         ],
-        out_specs=pl.BlockSpec((depth, chunk), lambda i: (0, i)),
-        compiler_params=pltpu.CompilerParams(vmem_limit_bytes=40 * 2**20),
+        out_specs=pl.BlockSpec((depth, chunk), lambda i: (0, jnp.maximum(i - 1, 0))),
+        scratch_shapes=[vmem((count, chunk), BF16)],
+        compiler_params=pltpu.CompilerParams(vmem_limit_bytes=60 * 2**20),
         name="grad",
     )(norm, nt, pre, gs, cot)
 

time: 78.8 us -> 63 us (0.80)
  Pallas kernels: 72.5 us -> 62.7 us
  local copies, waits for them, and re-layouts: 6.03 us -> 0 us
    pallas_call x1, Pallas kernels: 64.1 us -> 51.8 us  [per_device(): pl.pallas_call(functools.partial(slopes_kernel, cfg), out_shape=(jax.Shap...]
    unnamed x10 -> x0, local copies, waits for them, and re-layouts: 6.03 us -> none
    pallas_call x1, Pallas kernels: 8.4 us -> 10.9 us  [per_device(): pl.pallas_call(functools.partial(grad_kernel, count), grid=(chunks + 1,),...]
where the time goes in v2:
time: 63 us; the launch traced here: 62.7 us
  Pallas kernels  62.7 us (100%)
    pallas_call x1, Pallas kernels, per_device(): pl.pallas_call(functools.partial(slopes_kernel, cfg), out_shape=(jax.Shap...  51.8 us
    pallas_call x1, Pallas kernels, per_device(): pl.pallas_call(functools.partial(grad_kernel, count), grid=(chunks + 1,),...  10.9 us

profile of v2, /device:TPU:0, one launch (start us, length us, event | category | flops | bytes accessed | tf_op | source)
XLA Modules:
  0.0 62.7 jit_solution(9074222858985567014)
XLA Ops:
  0.0 51.8 %slopes.1 = (bf16[3072,256]{1,0:T(8,128)(2,1)}, f32[256,1536]{1,0:T(8,128)}, f32[256,1536]{1,0:T(8,128)}, bf16[256,1536]{1,0:T(8,128)(2,1)}, f32[8,128]{1,0:T(8,128)}) custom-call(bf16[16,3072]{1,0:T(8,128)(2,1)} %tok_ref.1, f32[1,3072]{1,0:T(1,128)} %bitcast.1, bf16[3072,1536]{1,0:T(8,128)(2,1)} %w_hbm.1, bf16[128,1536]{1,0:T(8,128)(2,1)} %cot_hbm.1), custom_call_target="tpu_custom_call" | custom-call | tf_op jit(solution)/shard_map/slopes/pallas_call | solution.py:385
  51.8 10.9 %grad.1 = f32[3072,1536]{1,0:T(8,128)} custom-call(f32[8,128]{1,0:T(8,128)} %get-tuple-element.10.norm_ref, bf16[3072,256]{1,0:T(8,128)(2,1)} %get-tuple-element.11.nt_ref, f32[256,1536]{1,0:T(8,128)} %get-tuple-element.12.pre_ref, f32[256,1536]{1,0:T(8,128)} %get-tuple-element.13.gs_ref, bf16[256,1536]{1,0:T(8,128)(2,1)} %get-tuple-element.14.cot_ref), custom_call_target="tpu_custom_call" | custom-call | tf_op jit(solution)/shard_map/grad/pallas_call | solution.py:429

commit v3 on v2

--- a/solution.py
+++ b/solution.py
@@ -30,11 +30,11 @@
 def slopes_kernel(
     cfg,
     tok_ref, gain_ref, w_hbm, cot_hbm,
-    nt_hbm, pre_hbm, gs_hbm, cot_out, norm_ref,
-    nt_ref, pre_ref, gs_ref, cot_ref, g_terms,
+    nt_hbm, slope_hbm,
+    nt_ref, pre_ref, gs_ref, cot_ref, g_terms, nlocal,
     xs, nall, w, st_part, st_part_in, st_all, own, sendb, recvb,
     g_part, g_part_in, g_all, slope, nb,
-    w_sem, c_sem, o_sem, pre_os, gs_os, z_ss, y_ss, core_ss, x_rs,
+    w_sem, c_sem, o_sem, slope_os, z_ss, y_ss, core_ss, x_rs,
     stp_ss, stp_rs, st_ss, st_rs, cot_ss, cot_rs, pre_ss, pre_rs,
     gp_ss, gp_rs, g_ss, g_rs, nb_ss, nb_rs,
 ):
@@ -51,6 +51,10 @@
     across = lax.rem(me // cores, per_line)
     along = me // (cores * per_line)
 
+    group = rows * cores
+    near = lines * group
+    parts = [(0, near), (near, token_count - near)]
+
     def index(a, b, c):
         return (a * per_line + b) * cores + c
 
@@ -173,12 +177,45 @@
     def normalize(src):
         x = xs[src].astype(F32)
         st = st_all[src]
-        value = (x - st[:, 0:1]) * st[:, 1:2] * gain_ref[...]
-        nall[pl.ds(pl.multiple_of(src * rows, rows), rows), :] = value.astype(BF16)
+        value = ((x - st[:, 0:1]) * st[:, 1:2] * gain_ref[...]).astype(BF16)
+        nall[pl.ds(pl.multiple_of(src * rows, rows), rows), :] = value
+        a = src // (cores * per_line)
+        p = lax.rem(lax.rem(src // cores, per_line) + per_line - across, per_line)
+        local = ((p * lines + a) * cores + lax.rem(src, cores)) * rows
+        nlocal[pl.ds(pl.multiple_of(local, rows), rows), :] = value
 
     @pl.loop(0, lines)
     def _(k):
         normalize(index(lax.rem(along + k, lines), across, core))
+
+    @pl.loop(0, lines)
+    def _(k):
+        src = index(lax.rem(along + k, lines), across, 1 - core)
+        arrived(src)
+        normalize(src)
+
+    w_copy.wait()
+
+    def pre_copy(part, i, k):
+        at, size = parts[part]
+        return remote(sendb.at[i, pl.ds(at, size)], recvb.at[my_mp, i, pl.ds(at, size)],
+                      pre_ss.at[part, i, k], pre_rs.at[part, my_mp, i], {"mp": mp_peer(k)})
+
+    def project(part, i):
+        at, size = parts[part]
+        off = pl.multiple_of(i * chunk, chunk)
+        value = jnp.dot(nlocal[pl.ds(at, size), :], w[:, pl.ds(off, chunk)],
+                        preferred_element_type=F32)
+        own[i, pl.ds(at, size)] = value
+        sendb[i, pl.ds(at, size)] = value.astype(BF16)
+        for k in range(1, m):
+            pre_copy(part, i, k).start()
+
+    first = min(2, chunks)
+
+    @pl.loop(0, first)
+    def _(i):
+        project(0, i)
 
     across_step(along)
     for pos, low in by_distance:
@@ -186,35 +223,23 @@
         def _():
             across_step(pos)
 
+    @pl.loop(first, chunks)
+    def _(i):
+        project(0, i)
+
     @pl.loop(0, lines * (per_line - 1))
     def _(i):
         k = i // (per_line - 1)
         j = 1 + lax.rem(i, per_line - 1)
         normalize(index(lax.rem(along + k, lines), lax.rem(across + j, per_line), core))
 
-    @pl.loop(0, lines * per_line)
-    def _(i):
-        k = i // per_line
-        j = lax.rem(i, per_line)
+    @pl.loop(0, lines * (per_line - 1))
+    def _(i):
+        k = i // (per_line - 1)
+        j = 1 + lax.rem(i, per_line - 1)
         src = index(lax.rem(along + k, lines), lax.rem(across + j, per_line), 1 - core)
         arrived(src)
         normalize(src)
-
-    w_copy.wait()
-
-    def pre_copy(i, k):
-        return remote(sendb.at[i], recvb.at[my_mp, i], pre_ss.at[i, k], pre_rs.at[my_mp, i],
-                      {"mp": mp_peer(k)})
-
-    def project(i):
-        off = pl.multiple_of(i * chunk, chunk)
-        part = jnp.dot(nall[...], w[:, pl.ds(off, chunk)], preferred_element_type=F32)
-        own[i] = part
-        sendb[i] = part.astype(BF16)
-        for k in range(1, m):
-            pre_copy(i, k).start()
-
-    project(0)
 
     mine = pl.ds(pl.multiple_of(me * rows, rows), rows)
     g_part[...] = lax.dot_general(
@@ -232,9 +257,49 @@
     for k in range(1, m):
         gp_copy(k).start()
 
-    @pl.loop(1, chunks)
-    def _(i):
-        project(i)
+    @pl.loop(0, chunks)
+    def _(i):
+        project(1, i)
+
+    @pl.loop(0, depth // 256)
+    def _(i):
+        off = pl.multiple_of(i * 256, 256)
+        nt_ref[pl.ds(off, 256), :] = nall[:, pl.ds(off, 256)].T
+
+    nt_copy = pltpu.make_async_copy(nt_ref, nt_hbm, o_sem.at[0])
+    nt_copy.start()
+
+    cot_copy.wait()
+    for k in range(1, m):
+        p = mp_peer(k)
+        dst = cot_ref.at[pl.ds(pl.multiple_of(p * cot_rows, cot_rows), cot_rows)]
+        remote(cot_hbm, dst, cot_ss.at[0], cot_rs.at[p], {"mp": p}).wait_recv()
+
+    def local_groups(part):
+        at, size = parts[part]
+        for g in range(at // group, (at + size) // group):
+            p, a = g // lines, g % lines
+            row = (a * per_line + lax.rem(across + p, per_line)) * group
+            yield pl.ds(pl.multiple_of(row, group), group)
+
+    def first_slopes(part, i):
+        at, size = parts[part]
+        off = pl.multiple_of(i * chunk, chunk)
+        pre = own[i, pl.ds(at, size)]
+        for k in range(1, m):
+            p = mp_peer(k)
+            remote(sendb.at[i, pl.ds(at, size)], recvb.at[p, i, pl.ds(at, size)],
+                   pre_ss.at[part, i, 0], pre_rs.at[part, p, i], {"mp": p}).wait_recv()
+            pre = pre + recvb[p, i, pl.ds(at, size)].astype(F32)
+        cot = jnp.concatenate([cot_ref[r, pl.ds(off, chunk)] for r in local_groups(part)], axis=0)
+        s = (cot.astype(F32) * gelu_slope(pre) * scale).astype(BF16)
+        for g, r in enumerate(local_groups(part)):
+            pre_ref[r, pl.ds(off, chunk)] = pre[g * group:(g + 1) * group]
+            slope[r, pl.ds(off, chunk)] = s[g * group:(g + 1) * group]
+
+    @pl.loop(0, chunks)
+    def _(i):
+        first_slopes(0, i)
 
     gram = g_part[...]
     for k in range(1, m):
@@ -247,61 +312,30 @@
     def _(k):
         g_copy(k).start()
 
-    @pl.loop(0, depth // 256)
-    def _(i):
-        off = pl.multiple_of(i * 256, 256)
-        nt_ref[pl.ds(off, 256), :] = nall[:, pl.ds(off, 256)].T
-
-    nt_copy = pltpu.make_async_copy(nt_ref, nt_hbm, o_sem.at[0])
-    nt_copy.start()
-
-    cot_copy.wait()
-    for k in range(1, m):
-        p = mp_peer(k)
-        dst = cot_ref.at[pl.ds(pl.multiple_of(p * cot_rows, cot_rows), cot_rows)]
-        remote(cot_hbm, dst, cot_ss.at[0], cot_rs.at[p], {"mp": p}).wait_recv()
-
     @pl.loop(1, n)
     def _(k):
         p = dp_peer(k)
         dst = g_all.at[pl.ds(pl.multiple_of(p * rows, rows), rows)]
         remote(dst, dst, g_ss.at[0], g_rs.at[p], {"dp": p}).wait_recv()
-
-    cot_write = pltpu.make_async_copy(cot_ref, cot_out, o_sem.at[1])
-    cot_write.start()
 
     rest = g_all[...]
     for t in range(3):
         g_terms[t] = rest.astype(BF16)
         rest = rest - g_terms[t].astype(F32)
 
-    def out_copy(i, buf, dst, sem):
-        cut = pl.ds(pl.multiple_of(i * chunk, chunk), chunk)
-        return pltpu.make_async_copy(buf.at[:, cut], dst.at[:, cut], sem.at[i])
-
     nb[me] = jnp.zeros_like(nb[me])
 
     @pl.loop(0, chunks)
     def _(i):
+        first_slopes(1, i)
         off = pl.multiple_of(i * chunk, chunk)
-        pre = own[i]
-        for k in range(1, m):
-            p = mp_peer(k)
-            remote(sendb.at[i], recvb.at[p, i], pre_ss.at[i, 0], pre_rs.at[p, i],
-                   {"mp": p}).wait_recv()
-            pre = pre + recvb[p, i].astype(F32)
-        pre_ref[:, pl.ds(off, chunk)] = pre
-        cot = cot_ref[:, pl.ds(off, chunk)].astype(F32)
-        slope[...] = (cot * gelu_slope(pre) * scale).astype(BF16)
-        out_copy(i, pre_ref, pre_hbm, pre_os).start()
-        s = slope[...]
+        s = slope[:, pl.ds(off, chunk)]
         gs = (
             jnp.dot(g_terms[2], s, preferred_element_type=F32)
             + jnp.dot(g_terms[1], s, preferred_element_type=F32)
             + jnp.dot(g_terms[0], s, preferred_element_type=F32)
         )
         gs_ref[:, pl.ds(off, chunk)] = gs
-        out_copy(i, gs_ref, gs_hbm, gs_os).start()
         nb[me] += jnp.full((8, 128), jnp.sum(gs * s.astype(F32)), F32)
 
     def nb_copy(k):
@@ -328,14 +362,6 @@
             if j > 0:
                 across_copy(pos, j).wait_send()
 
-    nt_copy.wait()
-    cot_write.wait()
-
-    @pl.loop(0, chunks)
-    def _(i):
-        out_copy(i, pre_ref, pre_hbm, pre_os).wait()
-        out_copy(i, gs_ref, gs_hbm, gs_os).wait()
-
     for k in range(1, m):
         stp_copy(k).wait_send()
         cot_send(k).wait_send()
@@ -343,7 +369,8 @@
 
         @pl.loop(0, chunks)
         def _(i):
-            pre_copy(i, k).wait_send()
+            pre_copy(0, i, k).wait_send()
+            pre_copy(1, i, k).wait_send()
 
     @pl.loop(1, n)
     def _(k):
@@ -351,21 +378,30 @@
         remote(nb.at[p], nb.at[p], nb_ss.at[0], nb_rs.at[p], {"dp": p}).wait_recv()
         nb_copy(k).wait_send()
 
-    norm_ref[...] = jnp.sum(nb[...], axis=0)
-
-
-def grad_kernel(token_count, norm_ref, nt_ref, pre_ref, gs_ref, cot_ref, out_ref, slope_ref):
-    @pl.when(pl.program_id(0) == 0)
-    def _():
-        slope_ref[...] = jnp.zeros_like(slope_ref)
-
-    before = slope_ref[...]
-    scale = 1.0 / math.sqrt(token_count)
-    size = jnp.sqrt(jnp.maximum(norm_ref[0:1, 0:1], 0.0)) + 1e-12
+    squared = jnp.sum(nb[...], axis=0)[0:1, 0:1]
+    size = jnp.sqrt(jnp.maximum(squared, 0.0)) + 1e-12
     radius = 0.5 * math.sqrt(FF)
-    pre = pre_ref[...] + radius * gs_ref[...] / size
-    out_ref[...] = jnp.dot(nt_ref[...], before, preferred_element_type=F32)
-    slope_ref[...] = (cot_ref[...].astype(F32) * gelu_slope(pre) * scale).astype(BF16)
+
+    def slope_copy(i):
+        at = pl.ds(pl.multiple_of(i * chunk, chunk), chunk)
+        return pltpu.make_async_copy(slope.at[:, at], slope_hbm.at[:, at], slope_os.at[i])
+
+    @pl.loop(0, chunks)
+    def _(i):
+        at = pl.ds(pl.multiple_of(i * chunk, chunk), chunk)
+        pre = pre_ref[:, at] + radius * gs_ref[:, at] / size
+        slope[:, at] = (cot_ref[:, at].astype(F32) * gelu_slope(pre) * scale).astype(BF16)
+        slope_copy(i).start()
+
+    nt_copy.wait()
+
+    @pl.loop(0, chunks)
+    def _(i):
+        slope_copy(i).wait()
+
+
+def grad_kernel(nt_ref, slope_ref, out_ref):
+    out_ref[...] = jnp.dot(nt_ref[...], slope_ref[...], preferred_element_type=F32)
 
 
 def per_device(tokens, norm_gain, w_up, cotangent):
@@ -382,23 +418,21 @@
     whole = pl.BlockSpec(memory_space=pltpu.VMEM)
     hbm = pl.BlockSpec(memory_space=pl.ANY)
     cfg = (n, m, lines, depth * m, count)
-    nt, pre, gs, cot, norm = pl.pallas_call(
+    nt, slope = pl.pallas_call(
         functools.partial(slopes_kernel, cfg),
         out_shape=(
             jax.ShapeDtypeStruct((depth, count), BF16),
-            jax.ShapeDtypeStruct((count, cols), F32),
-            jax.ShapeDtypeStruct((count, cols), F32),
             jax.ShapeDtypeStruct((count, cols), BF16),
-            jax.ShapeDtypeStruct((8, 128), F32),
         ),
         in_specs=[whole, whole, hbm, hbm],
-        out_specs=[hbm] * 4 + [whole],
+        out_specs=[hbm] * 2,
         scratch_shapes=[
             vmem((depth, count), BF16),
             vmem((count, cols), F32),
             vmem((count, cols), F32),
             vmem((count, cols), BF16),
             vmem((3, count, count), BF16),
+            vmem((count, depth), BF16),
             vmem((n, rows, depth), BF16),
             vmem((count, depth), BF16),
             vmem((depth, cols), BF16),
@@ -411,13 +445,13 @@
             vmem((rows, count), F32),
             vmem((m, rows, count), F32),
             vmem((count, count), F32),
-            vmem((count, chunk), BF16),
+            vmem((count, cols), BF16),
             vmem((n, 8, 128), F32),
-            dma(()), dma(()), dma((2,)), dma((chunks,)), dma((chunks,)),
+            dma(()), dma(()), dma((1,)), dma((chunks,)),
             dma((2, lines)), dma((lines, per_line)), dma((lines, per_line)),
             dma((n,)),
             dma((m,)), dma((m,)), dma((n,)), dma((n,)), dma((m,)), dma((m,)),
-            dma((chunks, m)), dma((m, chunks)),
+            dma((2, chunks, m)), dma((2, m, chunks)),
             dma((m,)), dma((m,)), dma((n,)), dma((n,)), dma((n,)), dma((n,)),
         ],
         compiler_params=pltpu.CompilerParams(
@@ -427,21 +461,17 @@
     )(tokens, norm_gain.reshape(1, depth), w_up, cotangent)
 
     return pl.pallas_call(
-        functools.partial(grad_kernel, count),
-        grid=(chunks + 1,),
+        grad_kernel,
+        grid=(depth // 256,),
         out_shape=jax.ShapeDtypeStruct((depth, cols), F32),
         in_specs=[
-            pl.BlockSpec((8, 128), lambda i: (0, 0)),
-            pl.BlockSpec((depth, count), lambda i: (0, 0)),
-            pl.BlockSpec((count, chunk), lambda i: (0, jnp.minimum(i, chunks - 1))),
-            pl.BlockSpec((count, chunk), lambda i: (0, jnp.minimum(i, chunks - 1))),
-            pl.BlockSpec((count, chunk), lambda i: (0, jnp.minimum(i, chunks - 1))),
+            pl.BlockSpec((256, count), lambda i: (i, 0)),
+            pl.BlockSpec((count, cols), lambda i: (0, 0)),
         ],
-        out_specs=pl.BlockSpec((depth, chunk), lambda i: (0, jnp.maximum(i - 1, 0))),
-        scratch_shapes=[vmem((count, chunk), BF16)],
+        out_specs=pl.BlockSpec((256, cols), lambda i: (i, 0)),
         compiler_params=pltpu.CompilerParams(vmem_limit_bytes=60 * 2**20),
         name="grad",
-    )(norm, nt, pre, gs, cot)
+    )(nt, slope)
 
 
 def solution(mesh):

time: 63 us -> 61.9 us (0.983)
  Pallas kernels: 62.7 us -> 61.5 us
    pallas_call x1, Pallas kernels: 51.8 us -> 49.6 us  [per_device(): pl.pallas_call(functools.partial(slopes_kernel, cfg), out_shape=(jax.Shap...]
    pallas_call x1, Pallas kernels: 10.9 us -> 12 us  [per_device(): pl.pallas_call(grad_kernel, grid=(depth // 256,), out_shape=jax.ShapeDtyp...]
where the time goes in v3:
time: 61.9 us; the launch traced here: 61.5 us
  Pallas kernels  61.5 us (99%)
    pallas_call x1, Pallas kernels, per_device(): pl.pallas_call(functools.partial(slopes_kernel, cfg), out_shape=(jax.Shap...  49.6 us
    pallas_call x1, Pallas kernels, per_device(): pl.pallas_call(grad_kernel, grid=(depth // 256,), out_shape=jax.ShapeDtyp...  12 us

profile of v3, /device:TPU:0, one launch (start us, length us, event | category | flops | bytes accessed | tf_op | source)
XLA Modules:
  0.0 61.5 jit_solution(18057201246645669881)
XLA Ops:
  0.0 49.6 %slopes.1 = (bf16[3072,256]{1,0:T(8,128)(2,1)}, bf16[256,1536]{1,0:T(8,128)(2,1)}) custom-call(bf16[16,3072]{1,0:T(8,128)(2,1)} %tok_ref.1, f32[1,3072]{1,0:T(1,128)} %bitcast.1, bf16[3072,1536]{1,0:T(8,128)(2,1)} %w_hbm.1, bf16[128,1536]{1,0:T(8,128)(2,1)} %cot_hbm.1), custom_call_target="tpu_custom_call" | custom-call | tf_op jit(solution)/shard_map/slopes/pallas_call | solution.py:421
  49.6 12.0 %grad.1 = f32[3072,1536]{1,0:T(8,128)} custom-call(bf16[3072,256]{1,0:T(8,128)(2,1)} %get-tuple-element.7.nt_ref, bf16[256,1536]{1,0:T(8,128)(2,1)} %get-tuple-element.8.slope_ref), custom_call_target="tpu_custom_call" | custom-call | tf_op jit(solution)/shard_map/grad/pallas_call | solution.py:463

commit v4 on v3

--- a/solution.py
+++ b/solution.py
@@ -129,6 +129,8 @@
 
     for k in range(1, m):
         stp_copy(k).start()
+    for k in range(1, m):
+        cot_send(k).start()
     for up in (True, False):
         @pl.when(can_go(up))
         def _():
@@ -142,8 +144,6 @@
         p = mp_peer(k)
         remote(st_part, st_part_in.at[p], stp_ss.at[0], stp_rs.at[p], {"mp": p}).wait_recv()
         total = total + st_part_in[p]
-    for k in range(1, m):
-        cot_send(k).start()
     mean = total[:, 0:1] / width_all
     var = total[:, 1:2] / width_all - mean * mean
     st_all[me] = jnp.where(lane == 0, mean, lax.rsqrt(var + 1e-06))
@@ -211,7 +211,7 @@
         for k in range(1, m):
             pre_copy(part, i, k).start()
 
-    first = min(2, chunks)
+    first = 1
 
     @pl.loop(0, first)
     def _(i):
@@ -410,7 +410,8 @@
     count = rows * n
     cols = w_up.shape[1]
     lines = 4
-    chunk = 256 if cols % 256 == 0 else 128
+    chunk = next(c for c in (512, 256, 128) if cols % c == 0)
+    narrow = min(chunk, 256)
     chunks = cols // chunk
     per_line = n // (2 * lines)
     cot_rows = cotangent.shape[0]
@@ -462,13 +463,13 @@
 
     return pl.pallas_call(
         grad_kernel,
-        grid=(depth // 256,),
+        grid=(2, cols // narrow),
         out_shape=jax.ShapeDtypeStruct((depth, cols), F32),
         in_specs=[
-            pl.BlockSpec((256, count), lambda i: (i, 0)),
-            pl.BlockSpec((count, cols), lambda i: (0, 0)),
+            pl.BlockSpec((depth // 2, count), lambda i, j: (i, 0)),
+            pl.BlockSpec((count, narrow), lambda i, j: (0, j)),
         ],
-        out_specs=pl.BlockSpec((256, cols), lambda i: (i, 0)),
+        out_specs=pl.BlockSpec((depth // 2, narrow), lambda i, j: (i, j)),
         compiler_params=pltpu.CompilerParams(vmem_limit_bytes=60 * 2**20),
         name="grad",
     )(nt, slope)

time: 61.9 us -> 61.3 us (level)
  no operation moved by 1% of the time
where the time goes in v4:
time: 61.3 us; the launch traced here: 61 us
  Pallas kernels  60.9 us (99%)
    pallas_call x1, Pallas kernels, per_device(): pl.pallas_call(functools.partial(slopes_kernel, cfg), out_shape=(jax.Shap...  49.1 us
    pallas_call x1, Pallas kernels, per_device(): pl.pallas_call(grad_kernel, grid=(2, cols // narrow), out_shape=jax.Shape...  11.9 us

profile of v4, /device:TPU:0, one launch (start us, length us, event | category | flops | bytes accessed | tf_op | source)
XLA Modules:
  0.0 61.0 jit_solution(16649427466541926628)
XLA Ops:
  0.0 49.1 %slopes.1 = (bf16[3072,256]{1,0:T(8,128)(2,1)}, bf16[256,1536]{1,0:T(8,128)(2,1)}) custom-call(bf16[16,3072]{1,0:T(8,128)(2,1)} %tok_ref.1, f32[1,3072]{1,0:T(1,128)} %bitcast.1, bf16[3072,1536]{1,0:T(8,128)(2,1)} %w_hbm.1, bf16[128,1536]{1,0:T(8,128)(2,1)} %cot_hbm.1), custom_call_target="tpu_custom_call" | custom-call | tf_op jit(solution)/shard_map/slopes/pallas_call | solution.py:422
  49.1 11.9 %grad.1 = f32[3072,1536]{1,0:T(8,128)} custom-call(bf16[3072,256]{1,0:T(8,128)(2,1)} %get-tuple-element.7.nt_ref, bf16[256,1536]{1,0:T(8,128)(2,1)} %get-tuple-element.8.slope_ref), custom_call_target="tpu_custom_call" | custom-call | tf_op jit(solution)/shard_map/grad/pallas_call | solution.py:464

commit v5 on v4

--- a/solution.py
+++ b/solution.py
@@ -139,6 +139,22 @@
         across_copy(along, j).start()
     core_copy(along, 0).start()
 
+    def relay(pos, low):
+        @pl.when(there(pos, low))
+        def _():
+            arrived(index(pos, across, core))
+
+            @pl.when(can_go(low))
+            def _():
+                line_copy(pos, low).start()
+
+            for j in range(1, per_line):
+                across_copy(pos, j).start()
+            core_copy(pos, 0).start()
+
+    for pos, low in by_distance[:2]:
+        relay(pos, low)
+
     total = st_part[...]
     for k in range(1, m):
         p = mp_peer(k)
@@ -156,18 +172,8 @@
     def _(k):
         st_copy(k).start()
 
-    for pos, low in by_distance:
-        @pl.when(there(pos, low))
-        def _():
-            arrived(index(pos, across, core))
-
-            @pl.when(can_go(low))
-            def _():
-                line_copy(pos, low).start()
-
-            for j in range(1, per_line):
-                across_copy(pos, j).start()
-            core_copy(pos, 0).start()
+    for pos, low in by_distance[2:]:
+        relay(pos, low)
 
     @pl.loop(1, n)
     def _(k):
@@ -261,13 +267,16 @@
     def _(i):
         project(1, i)
 
-    @pl.loop(0, depth // 256)
-    def _(i):
-        off = pl.multiple_of(i * 256, 256)
-        nt_ref[pl.ds(off, 256), :] = nall[:, pl.ds(off, 256)].T
-
-    nt_copy = pltpu.make_async_copy(nt_ref, nt_hbm, o_sem.at[0])
-    nt_copy.start()
+    gram = g_part[...]
+    for k in range(1, m):
+        p = mp_peer(k)
+        remote(g_part, g_part_in.at[p], gp_ss.at[0], gp_rs.at[p], {"mp": p}).wait_recv()
+        gram = gram + g_part_in[p]
+    g_all[mine, :] = gram
+
+    @pl.loop(1, n)
+    def _(k):
+        g_copy(k).start()
 
     cot_copy.wait()
     for k in range(1, m):
@@ -301,17 +310,6 @@
     def _(i):
         first_slopes(0, i)
 
-    gram = g_part[...]
-    for k in range(1, m):
-        p = mp_peer(k)
-        remote(g_part, g_part_in.at[p], gp_ss.at[0], gp_rs.at[p], {"mp": p}).wait_recv()
-        gram = gram + g_part_in[p]
-    g_all[mine, :] = gram
-
-    @pl.loop(1, n)
-    def _(k):
-        g_copy(k).start()
-
     @pl.loop(1, n)
     def _(k):
         p = dp_peer(k)
@@ -320,8 +318,9 @@
 
     rest = g_all[...]
     for t in range(3):
-        g_terms[t] = rest.astype(BF16)
-        rest = rest - g_terms[t].astype(F32)
+        term = rest.astype(BF16)
+        g_terms[t * token_count:(t + 1) * token_count] = term
+        rest = rest - term.astype(F32)
 
     nb[me] = jnp.zeros_like(nb[me])
 
@@ -330,11 +329,9 @@
         first_slopes(1, i)
         off = pl.multiple_of(i * chunk, chunk)
         s = slope[:, pl.ds(off, chunk)]
-        gs = (
-            jnp.dot(g_terms[2], s, preferred_element_type=F32)
-            + jnp.dot(g_terms[1], s, preferred_element_type=F32)
-            + jnp.dot(g_terms[0], s, preferred_element_type=F32)
-        )
+        terms = jnp.dot(g_terms[...], s, preferred_element_type=F32)
+        t = token_count
+        gs = terms[2 * t:] + terms[t:2 * t] + terms[:t]
         gs_ref[:, pl.ds(off, chunk)] = gs
         nb[me] += jnp.full((8, 128), jnp.sum(gs * s.astype(F32)), F32)
 
@@ -344,6 +341,14 @@
     @pl.loop(1, n)
     def _(k):
         nb_copy(k).start()
+
+    @pl.loop(0, depth // 256)
+    def _(i):
+        off = pl.multiple_of(i * 256, 256)
+        nt_ref[pl.ds(off, 256), :] = nall[:, pl.ds(off, 256)].T
+
+    nt_copy = pltpu.make_async_copy(nt_ref, nt_hbm, o_sem.at[0])
+    nt_copy.start()
 
     @pl.loop(1, n)
     def _(k):
@@ -400,8 +405,37 @@
         slope_copy(i).wait()
 
 
-def grad_kernel(nt_ref, slope_ref, out_ref):
-    out_ref[...] = jnp.dot(nt_ref[...], slope_ref[...], preferred_element_type=F32)
+def grad_kernel(nt_hbm, slope_hbm, out_hbm, nt, slope, out, nt_sem, slope_sem, out_sem):
+    blocks = nt_sem.shape[0]
+    rows = nt.shape[0] // blocks
+
+    def cut(i):
+        return pl.ds(pl.multiple_of(i * rows, rows), rows)
+
+    def nt_copy(i):
+        return pltpu.make_async_copy(nt_hbm.at[cut(i)], nt.at[cut(i)], nt_sem.at[i])
+
+    def out_copy(i):
+        return pltpu.make_async_copy(out.at[cut(i)], out_hbm.at[cut(i)], out_sem.at[i])
+
+    slope_copy = pltpu.make_async_copy(slope_hbm, slope, slope_sem)
+    slope_copy.start()
+
+    @pl.loop(0, blocks)
+    def _(i):
+        nt_copy(i).start()
+
+    slope_copy.wait()
+
+    @pl.loop(0, blocks)
+    def _(i):
+        nt_copy(i).wait()
+        out[cut(i), :] = jnp.dot(nt[cut(i), :], slope[...], preferred_element_type=F32)
+        out_copy(i).start()
+
+    @pl.loop(0, blocks)
+    def _(i):
+        out_copy(i).wait()
 
 
 def per_device(tokens, norm_gain, w_up, cotangent):
@@ -411,7 +445,6 @@
     cols = w_up.shape[1]
     lines = 4
     chunk = next(c for c in (512, 256, 128) if cols % c == 0)
-    narrow = min(chunk, 256)
     chunks = cols // chunk
     per_line = n // (2 * lines)
     cot_rows = cotangent.shape[0]
@@ -432,7 +465,7 @@
             vmem((count, cols), F32),
             vmem((count, cols), F32),
             vmem((count, cols), BF16),
-            vmem((3, count, count), BF16),
+            vmem((3 * count, count), BF16),
             vmem((count, depth), BF16),
             vmem((n, rows, depth), BF16),
             vmem((count, depth), BF16),
@@ -463,13 +496,15 @@
 
     return pl.pallas_call(
         grad_kernel,
-        grid=(2, cols // narrow),
         out_shape=jax.ShapeDtypeStruct((depth, cols), F32),
-        in_specs=[
-            pl.BlockSpec((depth // 2, count), lambda i, j: (i, 0)),
-            pl.BlockSpec((count, narrow), lambda i, j: (0, j)),
+        in_specs=[hbm, hbm],
+        out_specs=hbm,
+        scratch_shapes=[
+            vmem((depth, count), BF16),
+            vmem((count, cols), BF16),
+            vmem((depth, cols), F32),
+            dma((depth // 256,)), dma(()), dma((depth // 256,)),
         ],
-        out_specs=pl.BlockSpec((depth // 2, narrow), lambda i, j: (i, j)),
         compiler_params=pltpu.CompilerParams(vmem_limit_bytes=60 * 2**20),
         name="grad",
     )(nt, slope)

time: 61.3 us -> 58.5 us (0.954)
  Pallas kernels: 60.9 us -> 58.3 us
    pallas_call x1, Pallas kernels: 11.9 us -> 8.21 us  [per_device(): pl.pallas_call(grad_kernel, out_shape=jax.ShapeDtypeStruct((depth, cols),...]
    pallas_call x1, Pallas kernels: 49.1 us -> 50.1 us  [per_device(): pl.pallas_call(functools.partial(slopes_kernel, cfg), out_shape=(jax.Shap...]
where the time goes in v5:
time: 58.5 us; the launch traced here: 58.3 us
  Pallas kernels  58.3 us (100%)
    pallas_call x1, Pallas kernels, per_device(): pl.pallas_call(functools.partial(slopes_kernel, cfg), out_shape=(jax.Shap...  50.1 us
    pallas_call x1, Pallas kernels, per_device(): pl.pallas_call(grad_kernel, out_shape=jax.ShapeDtypeStruct((depth, cols),...  8.21 us

profile of v5, /device:TPU:0, one launch (start us, length us, event | category | flops | bytes accessed | tf_op | source)
XLA Modules:
  0.0 58.3 jit_solution(2387817451376057276)
XLA Ops:
  0.0 50.1 %slopes.1 = (bf16[3072,256]{1,0:T(8,128)(2,1)}, bf16[256,1536]{1,0:T(8,128)(2,1)}) custom-call(bf16[16,3072]{1,0:T(8,128)(2,1)} %tok_ref.1, f32[1,3072]{1,0:T(1,128)} %bitcast.1, bf16[3072,1536]{1,0:T(8,128)(2,1)} %w_hbm.1, bf16[128,1536]{1,0:T(8,128)(2,1)} %cot_hbm.1), custom_call_target="tpu_custom_call" | custom-call | tf_op jit(solution)/shard_map/slopes/pallas_call | solution.py:455
  50.1 8.2 %grad.1 = f32[3072,1536]{1,0:T(8,128)} custom-call(bf16[3072,256]{1,0:T(8,128)(2,1)} %get-tuple-element.7.nt_hbm, bf16[256,1536]{1,0:T(8,128)(2,1)} %get-tuple-element.8.slope_hbm), custom_call_target="tpu_custom_call" | custom-call | tf_op jit(solution)/shard_map/grad/pallas_call | solution.py:497

commit v6 on v5

--- a/solution.py
+++ b/solution.py
@@ -37,6 +37,7 @@
     w_sem, c_sem, o_sem, slope_os, z_ss, y_ss, core_ss, x_rs,
     stp_ss, stp_rs, st_ss, st_rs, cot_ss, cot_rs, pre_ss, pre_rs,
     gp_ss, gp_rs, g_ss, g_rs, nb_ss, nb_rs,
+    nx, cotx_ss, cotx_rs, nx_ss, nx_rs, sx_ss, sx_rs,
 ):
     n, m, lines, width_all, token_count = cfg
     rows, depth = tok_ref.shape
@@ -55,6 +56,13 @@
     near = lines * group
     parts = [(0, near), (near, token_count - near)]
 
+    split = m > 1 and chunk % (128 * m) == 0
+    shared = 1 if split else 0
+    share = chunk // m if split else chunk
+
+    def share_of(p):
+        return pl.ds(pl.multiple_of(p * share, share), share)
+
     def index(a, b, c):
         return (a * per_line + b) * cores + c
 
@@ -124,12 +132,25 @@
         return remote(st_part, st_part_in.at[my_mp], stp_ss.at[k], stp_rs.at[my_mp],
                       {"mp": mp_peer(k)})
 
+    rest_cols = pl.ds(shared * chunk, cols - shared * chunk)
+
+    def cot_rows_of(p):
+        return pl.ds(pl.multiple_of(p * cot_rows, cot_rows), cot_rows)
+
     def cot_send(k):
-        return remote(cot_hbm, cot_dst, cot_ss.at[k], cot_rs.at[my_mp], {"mp": mp_peer(k)})
+        return remote(cot_hbm.at[:, rest_cols], cot_ref.at[cot_rows_of(my_mp), rest_cols],
+                      cot_ss.at[k], cot_rs.at[my_mp], {"mp": mp_peer(k)})
+
+    def cot_send_shared(k):
+        at = share_of(mp_peer(k))
+        return remote(cot_hbm.at[:, at], cot_ref.at[cot_rows_of(my_mp), at],
+                      cotx_ss.at[k], cotx_rs.at[my_mp], {"mp": mp_peer(k)})
 
     for k in range(1, m):
         stp_copy(k).start()
     for k in range(1, m):
+        if split:
+            cot_send_shared(k).start()
         cot_send(k).start()
     for up in (True, False):
         @pl.when(can_go(up))
@@ -207,7 +228,13 @@
         return remote(sendb.at[i, pl.ds(at, size)], recvb.at[my_mp, i, pl.ds(at, size)],
                       pre_ss.at[part, i, k], pre_rs.at[part, my_mp, i], {"mp": mp_peer(k)})
 
-    def project(part, i):
+    def shared_copy(part, k):
+        rows_at = pl.ds(*parts[part])
+        at = share_of(mp_peer(k))
+        return remote(sendb.at[0, rows_at, at], recvb.at[my_mp, 0, rows_at, at],
+                      pre_ss.at[part, 0, k], pre_rs.at[part, my_mp, 0], {"mp": mp_peer(k)})
+
+    def project(part, i, copy=pre_copy):
         at, size = parts[part]
         off = pl.multiple_of(i * chunk, chunk)
         value = jnp.dot(nlocal[pl.ds(at, size), :], w[:, pl.ds(off, chunk)],
@@ -215,13 +242,16 @@
         own[i, pl.ds(at, size)] = value
         sendb[i, pl.ds(at, size)] = value.astype(BF16)
         for k in range(1, m):
-            pre_copy(part, i, k).start()
+            copy(part, i, k).start()
+
+    def project_first(part):
+        if split:
+            project(part, 0, lambda part, i, k: shared_copy(part, k))
+        else:
+            project(part, 0)
 
     first = 1
-
-    @pl.loop(0, first)
-    def _(i):
-        project(0, i)
+    project_first(0)
 
     across_step(along)
     for pos, low in by_distance:
@@ -263,7 +293,9 @@
     for k in range(1, m):
         gp_copy(k).start()
 
-    @pl.loop(0, chunks)
+    project_first(1)
+
+    @pl.loop(1, chunks)
     def _(i):
         project(1, i)
 
@@ -281,8 +313,12 @@
     cot_copy.wait()
     for k in range(1, m):
         p = mp_peer(k)
-        dst = cot_ref.at[pl.ds(pl.multiple_of(p * cot_rows, cot_rows), cot_rows)]
-        remote(cot_hbm, dst, cot_ss.at[0], cot_rs.at[p], {"mp": p}).wait_recv()
+        remote(cot_hbm.at[:, rest_cols], cot_ref.at[cot_rows_of(p), rest_cols],
+               cot_ss.at[0], cot_rs.at[p], {"mp": p}).wait_recv()
+        if split:
+            at = share_of(my_mp)
+            remote(cot_hbm.at[:, at], cot_ref.at[cot_rows_of(p), at],
+                   cotx_ss.at[0], cotx_rs.at[p], {"mp": p}).wait_recv()
 
     def local_groups(part):
         at, size = parts[part]
@@ -291,24 +327,35 @@
             row = (a * per_line + lax.rem(across + p, per_line)) * group
             yield pl.ds(pl.multiple_of(row, group), group)
 
-    def first_slopes(part, i):
-        at, size = parts[part]
-        off = pl.multiple_of(i * chunk, chunk)
-        pre = own[i, pl.ds(at, size)]
+    def first_slopes(part, i, inside, off, width):
+        rows_at = pl.ds(*parts[part])
+        at = pl.ds(off, width)
+        pre = own[i, rows_at, inside]
         for k in range(1, m):
             p = mp_peer(k)
-            remote(sendb.at[i, pl.ds(at, size)], recvb.at[p, i, pl.ds(at, size)],
+            remote(sendb.at[i, rows_at, inside], recvb.at[p, i, rows_at, inside],
                    pre_ss.at[part, i, 0], pre_rs.at[part, p, i], {"mp": p}).wait_recv()
-            pre = pre + recvb[p, i, pl.ds(at, size)].astype(F32)
-        cot = jnp.concatenate([cot_ref[r, pl.ds(off, chunk)] for r in local_groups(part)], axis=0)
+            pre = pre + recvb[p, i, rows_at, inside].astype(F32)
+        cot = jnp.concatenate([cot_ref[r, at] for r in local_groups(part)], axis=0)
         s = (cot.astype(F32) * gelu_slope(pre) * scale).astype(BF16)
         for g, r in enumerate(local_groups(part)):
-            pre_ref[r, pl.ds(off, chunk)] = pre[g * group:(g + 1) * group]
-            slope[r, pl.ds(off, chunk)] = s[g * group:(g + 1) * group]
-
-    @pl.loop(0, chunks)
-    def _(i):
-        first_slopes(0, i)
+            pre_ref[r, at] = pre[g * group:(g + 1) * group]
+            slope[r, at] = s[g * group:(g + 1) * group]
+
+    mine_off = pl.multiple_of(my_mp * share, share)
+
+    def shared_slopes(part):
+        first_slopes(part, 0, share_of(my_mp), mine_off, share)
+
+    def whole_slopes(part, i):
+        first_slopes(part, i, pl.ds(0, chunk), pl.multiple_of(i * chunk, chunk), chunk)
+
+    if split:
+        shared_slopes(0)
+
+    @pl.loop(shared, chunks)
+    def _(i):
+        whole_slopes(0, i)
 
     @pl.loop(1, n)
     def _(k):
@@ -322,18 +369,35 @@
         g_terms[t * token_count:(t + 1) * token_count] = term
         rest = rest - term.astype(F32)
 
-    nb[me] = jnp.zeros_like(nb[me])
-
-    @pl.loop(0, chunks)
-    def _(i):
-        first_slopes(1, i)
-        off = pl.multiple_of(i * chunk, chunk)
-        s = slope[:, pl.ds(off, chunk)]
+    def ascent(at):
+        s = slope[:, at]
         terms = jnp.dot(g_terms[...], s, preferred_element_type=F32)
         t = token_count
         gs = terms[2 * t:] + terms[t:2 * t] + terms[:t]
-        gs_ref[:, pl.ds(off, chunk)] = gs
-        nb[me] += jnp.full((8, 128), jnp.sum(gs * s.astype(F32)), F32)
+        gs_ref[:, at] = gs
+        return jnp.full((8, 128), jnp.sum(gs * s.astype(F32)), F32)
+
+    def nx_copy(k):
+        return remote(nx.at[my_mp], nx.at[my_mp], nx_ss.at[k], nx_rs.at[my_mp],
+                      {"mp": mp_peer(k)})
+
+    nb[me] = jnp.zeros_like(nb[me])
+    if split:
+        shared_slopes(1)
+        nx[my_mp] = ascent(pl.ds(mine_off, share))
+        for k in range(1, m):
+            nx_copy(k).start()
+
+    @pl.loop(shared, chunks)
+    def _(i):
+        whole_slopes(1, i)
+        nb[me] += ascent(pl.ds(pl.multiple_of(i * chunk, chunk), chunk))
+
+    if split:
+        for k in range(1, m):
+            p = mp_peer(k)
+            remote(nx.at[p], nx.at[p], nx_ss.at[0], nx_rs.at[p], {"mp": p}).wait_recv()
+        nb[me] += jnp.sum(nx[...], axis=0)
 
     def nb_copy(k):
         return remote(nb.at[me], nb.at[me], nb_ss.at[k], nb_rs.at[me], {"dp": dp_peer(k)})
@@ -372,7 +436,13 @@
         cot_send(k).wait_send()
         gp_copy(k).wait_send()
 
-        @pl.loop(0, chunks)
+        if split:
+            cot_send_shared(k).wait_send()
+            shared_copy(0, k).wait_send()
+            shared_copy(1, k).wait_send()
+            nx_copy(k).wait_send()
+
+        @pl.loop(shared, chunks)
         def _(i):
             pre_copy(0, i, k).wait_send()
             pre_copy(1, i, k).wait_send()
@@ -391,12 +461,33 @@
         at = pl.ds(pl.multiple_of(i * chunk, chunk), chunk)
         return pltpu.make_async_copy(slope.at[:, at], slope_hbm.at[:, at], slope_os.at[i])
 
-    @pl.loop(0, chunks)
-    def _(i):
-        at = pl.ds(pl.multiple_of(i * chunk, chunk), chunk)
+    def second_slopes(at):
         pre = pre_ref[:, at] + radius * gs_ref[:, at] / size
         slope[:, at] = (cot_ref[:, at].astype(F32) * gelu_slope(pre) * scale).astype(BF16)
+
+    def sx_copy(k):
+        at = pl.ds(mine_off, share)
+        return remote(slope.at[:, at], slope.at[:, at], sx_ss.at[k], sx_rs.at[my_mp],
+                      {"mp": mp_peer(k)})
+
+    if split:
+        second_slopes(pl.ds(mine_off, share))
+        for k in range(1, m):
+            sx_copy(k).start()
+
+    @pl.loop(shared, chunks)
+    def _(i):
+        second_slopes(pl.ds(pl.multiple_of(i * chunk, chunk), chunk))
         slope_copy(i).start()
+
+    if split:
+        for k in range(1, m):
+            p = mp_peer(k)
+            at = share_of(p)
+            remote(slope.at[:, at], slope.at[:, at], sx_ss.at[0], sx_rs.at[p], {"mp": p}).wait_recv()
+        slope_copy(0).start()
+        for k in range(1, m):
+            sx_copy(k).wait_send()
 
     nt_copy.wait()
 
@@ -487,6 +578,8 @@
             dma((m,)), dma((m,)), dma((n,)), dma((n,)), dma((m,)), dma((m,)),
             dma((2, chunks, m)), dma((2, m, chunks)),
             dma((m,)), dma((m,)), dma((n,)), dma((n,)), dma((n,)), dma((n,)),
+            vmem((m, 8, 128), F32),
+            dma((m,)), dma((m,)), dma((m,)), dma((m,)), dma((m,)), dma((m,)),
         ],
         compiler_params=pltpu.CompilerParams(
             collective_id=0, has_side_effects=True, vmem_limit_bytes=56 * 2**20

time: 58.5 us -> 61.2 us (1.046)
  Pallas kernels: 58.3 us -> 61 us
    pallas_call x1, Pallas kernels: 50.1 us -> 52.8 us  [per_device(): pl.pallas_call(functools.partial(slopes_kernel, cfg), out_shape=(jax.Shap...]
where the time goes in v6:
time: 61.2 us; the launch traced here: 61 us
  Pallas kernels  61 us (100%)
    pallas_call x1, Pallas kernels, per_device(): pl.pallas_call(functools.partial(slopes_kernel, cfg), out_shape=(jax.Shap...  52.8 us
    pallas_call x1, Pallas kernels, per_device(): pl.pallas_call(grad_kernel, out_shape=jax.ShapeDtypeStruct((depth, cols),...  8.21 us

profile of v6, /device:TPU:0, one launch (start us, length us, event | category | flops | bytes accessed | tf_op | source)
XLA Modules:
  0.0 61.0 jit_solution(18091435382832245365)
XLA Ops:
  0.0 52.8 %slopes.1 = (bf16[3072,256]{1,0:T(8,128)(2,1)}, bf16[256,1536]{1,0:T(8,128)(2,1)}) custom-call(bf16[16,3072]{1,0:T(8,128)(2,1)} %tok_ref.1, f32[1,3072]{1,0:T(1,128)} %bitcast.1, bf16[3072,1536]{1,0:T(8,128)(2,1)} %w_hbm.1, bf16[128,1536]{1,0:T(8,128)(2,1)} %cot_hbm.1), custom_call_target="tpu_custom_call" | custom-call | tf_op jit(solution)/shard_map/slopes/pallas_call | solution.py:546
  52.8 8.2 %grad.1 = f32[3072,1536]{1,0:T(8,128)} custom-call(bf16[3072,256]{1,0:T(8,128)(2,1)} %get-tuple-element.7.nt_hbm, bf16[256,1536]{1,0:T(8,128)(2,1)} %get-tuple-element.8.slope_hbm), custom_call_target="tpu_custom_call" | custom-call | tf_op jit(solution)/shard_map/grad/pallas_call | solution.py:590

commit v7 on v5

--- a/solution.py
+++ b/solution.py
@@ -30,11 +30,11 @@
 def slopes_kernel(
     cfg,
     tok_ref, gain_ref, w_hbm, cot_hbm,
-    nt_hbm, slope_hbm,
+    nt_hbm, pre_hbm, gs_hbm, cot_out, norm_ref,
     nt_ref, pre_ref, gs_ref, cot_ref, g_terms, nlocal,
     xs, nall, w, st_part, st_part_in, st_all, own, sendb, recvb,
     g_part, g_part_in, g_all, slope, nb,
-    w_sem, c_sem, o_sem, slope_os, z_ss, y_ss, core_ss, x_rs,
+    w_sem, c_sem, o_sem, pre_os, gs_os, z_ss, y_ss, core_ss, x_rs,
     stp_ss, stp_rs, st_ss, st_rs, cot_ss, cot_rs, pre_ss, pre_rs,
     gp_ss, gp_rs, g_ss, g_rs, nb_ss, nb_rs,
 ):
@@ -284,6 +284,13 @@
         dst = cot_ref.at[pl.ds(pl.multiple_of(p * cot_rows, cot_rows), cot_rows)]
         remote(cot_hbm, dst, cot_ss.at[0], cot_rs.at[p], {"mp": p}).wait_recv()
 
+    cot_write = pltpu.make_async_copy(cot_ref, cot_out, o_sem.at[1])
+    cot_write.start()
+
+    def out_copy(i, buf, dst, sem):
+        at = pl.ds(pl.multiple_of(i * chunk, chunk), chunk)
+        return pltpu.make_async_copy(buf.at[:, at], dst.at[:, at], sem.at[i])
+
     def local_groups(part):
         at, size = parts[part]
         for g in range(at // group, (at + size) // group):
@@ -327,12 +334,14 @@
     @pl.loop(0, chunks)
     def _(i):
         first_slopes(1, i)
+        out_copy(i, pre_ref, pre_hbm, pre_os).start()
         off = pl.multiple_of(i * chunk, chunk)
         s = slope[:, pl.ds(off, chunk)]
         terms = jnp.dot(g_terms[...], s, preferred_element_type=F32)
         t = token_count
         gs = terms[2 * t:] + terms[t:2 * t] + terms[:t]
         gs_ref[:, pl.ds(off, chunk)] = gs
+        out_copy(i, gs_ref, gs_hbm, gs_os).start()
         nb[me] += jnp.full((8, 128), jnp.sum(gs * s.astype(F32)), F32)
 
     def nb_copy(k):
@@ -383,59 +392,74 @@
         remote(nb.at[p], nb.at[p], nb_ss.at[0], nb_rs.at[p], {"dp": p}).wait_recv()
         nb_copy(k).wait_send()
 
-    squared = jnp.sum(nb[...], axis=0)[0:1, 0:1]
-    size = jnp.sqrt(jnp.maximum(squared, 0.0)) + 1e-12
+    norm_ref[...] = jnp.sum(nb[...], axis=0)
+    nt_copy.wait()
+    cot_write.wait()
+
+    @pl.loop(0, chunks)
+    def _(i):
+        out_copy(i, pre_ref, pre_hbm, pre_os).wait()
+        out_copy(i, gs_ref, gs_hbm, gs_os).wait()
+
+
+def grad_kernel(
+    token_count, norm_ref, nt_hbm, pre_hbm, gs_hbm, cot_hbm, out_hbm,
+    nt, pre, gs, cot, slope, out, nt_sem, in_sem, out_sem,
+):
+    chunks, blocks = out_sem.shape
+    rows = nt.shape[0] // blocks
+    narrow = slope.shape[1]
+
+    def down(i):
+        return pl.ds(pl.multiple_of(i * rows, rows), rows)
+
+    def inputs(j):
+        at = pl.ds(j * narrow, narrow)
+        pairs = ((pre_hbm, pre), (gs_hbm, gs), (cot_hbm, cot))
+        return [
+            pltpu.make_async_copy(src.at[:, at], dst.at[:, at], in_sem.at[k, j])
+            for k, (src, dst) in enumerate(pairs)
+        ]
+
+    def nt_copy(i):
+        return pltpu.make_async_copy(nt_hbm.at[down(i)], nt.at[down(i)], nt_sem.at[i])
+
+    def out_copy(i, j):
+        at = pl.ds(j * narrow, narrow)
+        return pltpu.make_async_copy(out.at[down(i), at], out_hbm.at[down(i), at], out_sem.at[j, i])
+
+    for copy in inputs(0):
+        copy.start()
+
+    @pl.loop(0, blocks)
+    def _(i):
+        nt_copy(i).start()
+
+    for j in range(1, chunks):
+        for copy in inputs(j):
+            copy.start()
+
+    scale = 1.0 / math.sqrt(token_count)
+    size = jnp.sqrt(jnp.maximum(norm_ref[0:1, 0:1], 0.0)) + 1e-12
     radius = 0.5 * math.sqrt(FF)
-
-    def slope_copy(i):
-        at = pl.ds(pl.multiple_of(i * chunk, chunk), chunk)
-        return pltpu.make_async_copy(slope.at[:, at], slope_hbm.at[:, at], slope_os.at[i])
-
-    @pl.loop(0, chunks)
-    def _(i):
-        at = pl.ds(pl.multiple_of(i * chunk, chunk), chunk)
-        pre = pre_ref[:, at] + radius * gs_ref[:, at] / size
-        slope[:, at] = (cot_ref[:, at].astype(F32) * gelu_slope(pre) * scale).astype(BF16)
-        slope_copy(i).start()
-
-    nt_copy.wait()
-
-    @pl.loop(0, chunks)
-    def _(i):
-        slope_copy(i).wait()
-
-
-def grad_kernel(nt_hbm, slope_hbm, out_hbm, nt, slope, out, nt_sem, slope_sem, out_sem):
-    blocks = nt_sem.shape[0]
-    rows = nt.shape[0] // blocks
-
-    def cut(i):
-        return pl.ds(pl.multiple_of(i * rows, rows), rows)
-
-    def nt_copy(i):
-        return pltpu.make_async_copy(nt_hbm.at[cut(i)], nt.at[cut(i)], nt_sem.at[i])
-
-    def out_copy(i):
-        return pltpu.make_async_copy(out.at[cut(i)], out_hbm.at[cut(i)], out_sem.at[i])
-
-    slope_copy = pltpu.make_async_copy(slope_hbm, slope, slope_sem)
-    slope_copy.start()
-
-    @pl.loop(0, blocks)
-    def _(i):
-        nt_copy(i).start()
-
-    slope_copy.wait()
-
-    @pl.loop(0, blocks)
-    def _(i):
-        nt_copy(i).wait()
-        out[cut(i), :] = jnp.dot(nt[cut(i), :], slope[...], preferred_element_type=F32)
-        out_copy(i).start()
-
-    @pl.loop(0, blocks)
-    def _(i):
-        out_copy(i).wait()
+    for j in range(chunks):
+        at = pl.ds(j * narrow, narrow)
+        for copy in inputs(j):
+            copy.wait()
+        perturbed = pre[:, at] + radius * gs[:, at] / size
+        slope[...] = (cot[:, at].astype(F32) * gelu_slope(perturbed) * scale).astype(BF16)
+
+        @pl.loop(0, blocks)
+        def _(i):
+            if j == 0:
+                nt_copy(i).wait()
+            out[down(i), at] = jnp.dot(nt[down(i), :], slope[...], preferred_element_type=F32)
+            out_copy(i, j).start()
+
+    for j in range(chunks):
+        @pl.loop(0, blocks)
+        def _(i):
+            out_copy(i, j).wait()
 
 
 def per_device(tokens, norm_gain, w_up, cotangent):
@@ -447,19 +471,24 @@
     chunk = next(c for c in (512, 256, 128) if cols % c == 0)
     chunks = cols // chunk
     per_line = n // (2 * lines)
+    narrow = min(chunk, 256)
+    blocks = next(b for b in (4, 2, 1) if depth % (b * 16) == 0)
     cot_rows = cotangent.shape[0]
     dma, vmem = pltpu.SemaphoreType.DMA, pltpu.VMEM
     whole = pl.BlockSpec(memory_space=pltpu.VMEM)
     hbm = pl.BlockSpec(memory_space=pl.ANY)
     cfg = (n, m, lines, depth * m, count)
-    nt, slope = pl.pallas_call(
+    nt, pre, gs, cot, norm = pl.pallas_call(
         functools.partial(slopes_kernel, cfg),
         out_shape=(
             jax.ShapeDtypeStruct((depth, count), BF16),
+            jax.ShapeDtypeStruct((count, cols), F32),
+            jax.ShapeDtypeStruct((count, cols), F32),
             jax.ShapeDtypeStruct((count, cols), BF16),
+            jax.ShapeDtypeStruct((8, 128), F32),
         ),
         in_specs=[whole, whole, hbm, hbm],
-        out_specs=[hbm] * 2,
+        out_specs=[hbm] * 4 + [whole],
         scratch_shapes=[
             vmem((depth, count), BF16),
             vmem((count, cols), F32),
@@ -481,7 +510,7 @@
             vmem((count, count), F32),
             vmem((count, cols), BF16),
             vmem((n, 8, 128), F32),
-            dma(()), dma(()), dma((1,)), dma((chunks,)),
+            dma(()), dma(()), dma((2,)), dma((chunks,)), dma((chunks,)),
             dma((2, lines)), dma((lines, per_line)), dma((lines, per_line)),
             dma((n,)),
             dma((m,)), dma((m,)), dma((n,)), dma((n,)), dma((m,)), dma((m,)),
@@ -495,19 +524,22 @@
     )(tokens, norm_gain.reshape(1, depth), w_up, cotangent)
 
     return pl.pallas_call(
-        grad_kernel,
+        functools.partial(grad_kernel, count),
         out_shape=jax.ShapeDtypeStruct((depth, cols), F32),
-        in_specs=[hbm, hbm],
+        in_specs=[whole] + [hbm] * 4,
         out_specs=hbm,
         scratch_shapes=[
             vmem((depth, count), BF16),
+            vmem((count, cols), F32),
+            vmem((count, cols), F32),
             vmem((count, cols), BF16),
+            vmem((count, narrow), BF16),
             vmem((depth, cols), F32),
-            dma((depth // 256,)), dma(()), dma((depth // 256,)),
+            dma((blocks,)), dma((3, cols // narrow)), dma((cols // narrow, blocks)),
         ],
         compiler_params=pltpu.CompilerParams(vmem_limit_bytes=60 * 2**20),
         name="grad",
-    )(nt, slope)
+    )(norm, nt, pre, gs, cot)
 
 
 def solution(mesh):

time: 58.5 us -> 59.1 us (1.010)
  Pallas kernels: 58.3 us -> 58.9 us
    pallas_call x1, Pallas kernels: 8.21 us -> 10.4 us  [per_device(): pl.pallas_call(functools.partial(grad_kernel, count), out_shape=jax.Shape...]
    pallas_call x1, Pallas kernels: 50.1 us -> 48.5 us  [per_device(): pl.pallas_call(functools.partial(slopes_kernel, cfg), out_shape=(jax.Shap...]
where the time goes in v7:
time: 59.1 us; the launch traced here: 58.9 us
  Pallas kernels  58.9 us (100%)
    pallas_call x1, Pallas kernels, per_device(): pl.pallas_call(functools.partial(slopes_kernel, cfg), out_shape=(jax.Shap...  48.5 us
    pallas_call x1, Pallas kernels, per_device(): pl.pallas_call(functools.partial(grad_kernel, count), out_shape=jax.Shape...  10.4 us

profile of v7, /device:TPU:0, one launch (start us, length us, event | category | flops | bytes accessed | tf_op | source)
XLA Modules:
  0.0 58.9 jit_solution(7023841508590069683)
XLA Ops:
  0.0 48.5 %slopes.1 = (bf16[3072,256]{1,0:T(8,128)(2,1)}, f32[256,1536]{1,0:T(8,128)}, f32[256,1536]{1,0:T(8,128)}, bf16[256,1536]{1,0:T(8,128)(2,1)}, f32[8,128]{1,0:T(8,128)}) custom-call(bf16[16,3072]{1,0:T(8,128)(2,1)} %tok_ref.1, f32[1,3072]{1,0:T(1,128)} %bitcast.1, bf16[3072,1536]{1,0:T(8,128)(2,1)} %w_hbm.1, bf16[128,1536]{1,0:T(8,128)(2,1)} %cot_hbm.1), custom_call_target="tpu_custom_call" | custom-call | tf_op jit(solution)/shard_map/slopes/pallas_call | solution.py:481
  48.5 10.4 %grad.1 = f32[3072,1536]{1,0:T(8,128)} custom-call(f32[8,128]{1,0:T(8,128)} %get-tuple-element.10.norm_ref, bf16[3072,256]{1,0:T(8,128)(2,1)} %get-tuple-element.11.nt_hbm, f32[256,1536]{1,0:T(8,128)} %get-tuple-element.12.pre_hbm, f32[256,1536]{1,0:T(8,128)} %get-tuple-element.13.gs_hbm, bf16[256,1536]{1,0:T(8,128)(2,1)} %get-tuple-element.14.cot_hbm), custom_call_target="tpu_custom_call" | custom-call | tf_op jit(solution)/shard_map/grad/pallas_call | solution.py:526

commit v8 on v5

--- a/solution.py
+++ b/solution.py
@@ -267,17 +267,6 @@
     def _(i):
         project(1, i)
 
-    gram = g_part[...]
-    for k in range(1, m):
-        p = mp_peer(k)
-        remote(g_part, g_part_in.at[p], gp_ss.at[0], gp_rs.at[p], {"mp": p}).wait_recv()
-        gram = gram + g_part_in[p]
-    g_all[mine, :] = gram
-
-    @pl.loop(1, n)
-    def _(k):
-        g_copy(k).start()
-
     cot_copy.wait()
     for k in range(1, m):
         p = mp_peer(k)
@@ -310,6 +299,17 @@
     def _(i):
         first_slopes(0, i)
 
+    gram = g_part[...]
+    for k in range(1, m):
+        p = mp_peer(k)
+        remote(g_part, g_part_in.at[p], gp_ss.at[0], gp_rs.at[p], {"mp": p}).wait_recv()
+        gram = gram + g_part_in[p]
+    g_all[mine, :] = gram
+
+    @pl.loop(1, n)
+    def _(k):
+        g_copy(k).start()
+
     @pl.loop(1, n)
     def _(k):
         p = dp_peer(k)
@@ -329,9 +329,12 @@
         first_slopes(1, i)
         off = pl.multiple_of(i * chunk, chunk)
         s = slope[:, pl.ds(off, chunk)]
-        terms = jnp.dot(g_terms[...], s, preferred_element_type=F32)
         t = token_count
-        gs = terms[2 * t:] + terms[t:2 * t] + terms[:t]
+        gs = (
+            jnp.dot(g_terms[2 * t:], s, preferred_element_type=F32)
+            + jnp.dot(g_terms[t:2 * t], s, preferred_element_type=F32)
+            + jnp.dot(g_terms[:t], s, preferred_element_type=F32)
+        )
         gs_ref[:, pl.ds(off, chunk)] = gs
         nb[me] += jnp.full((8, 128), jnp.sum(gs * s.astype(F32)), F32)
 

time: 58.5 us -> 58.5 us (level)
  no operation moved by 1% of the time
where the time goes in v8:
time: 58.5 us; the launch traced here: 58.3 us
  Pallas kernels  58.3 us (100%)
    pallas_call x1, Pallas kernels, per_device(): pl.pallas_call(functools.partial(slopes_kernel, cfg), out_shape=(jax.Shap...  50.1 us
    pallas_call x1, Pallas kernels, per_device(): pl.pallas_call(grad_kernel, out_shape=jax.ShapeDtypeStruct((depth, cols),...  8.21 us

profile of v8, /device:TPU:0, one launch (start us, length us, event | category | flops | bytes accessed | tf_op | source)
XLA Modules:
  0.0 58.3 jit_solution(7896619152411621987)
XLA Ops:
  0.0 50.1 %slopes.1 = (bf16[3072,256]{1,0:T(8,128)(2,1)}, bf16[256,1536]{1,0:T(8,128)(2,1)}) custom-call(bf16[16,3072]{1,0:T(8,128)(2,1)} %tok_ref.1, f32[1,3072]{1,0:T(1,128)} %bitcast.1, bf16[3072,1536]{1,0:T(8,128)(2,1)} %w_hbm.1, bf16[128,1536]{1,0:T(8,128)(2,1)} %cot_hbm.1), custom_call_target="tpu_custom_call" | custom-call | tf_op jit(solution)/shard_map/slopes/pallas_call | solution.py:458
  50.1 8.2 %grad.1 = f32[3072,1536]{1,0:T(8,128)} custom-call(bf16[3072,256]{1,0:T(8,128)(2,1)} %get-tuple-element.7.nt_hbm, bf16[256,1536]{1,0:T(8,128)(2,1)} %get-tuple-element.8.slope_hbm), custom_call_target="tpu_custom_call" | custom-call | tf_op jit(solution)/shard_map/grad/pallas_call | solution.py:500
